TPU v7x, 32 devices: a whole 2x2x4 slice. The times are simulated.
32 devices in a mesh: tile: 16 (over z, x, core), pgrp: 2 (over y).
Axes of the slice: x: 2, y: 2, z: 4, core: 2. Of those that a mesh axis runs over, the one named last changes fastest.
Arguments:
- concentrations: float32 [130, 16, 256], P(None, 'tile'), may hold values from 0.1 to 2
- tangents: float32 [64, 130, 16, 256], P('pgrp', None, 'tile'), may hold values from -6 to 6
- rates: float32 [218, 16, 256], P(None, 'tile'), may hold values from 0.01 to 1
- substeps: int32 [16, 256], P('tile'), may hold values from 1 to 4, as said below
- courant: float32 [2, 16, 256], P(None, 'tile'), may hold values from -0.9 to 0.9
- reactants: int32 [218, 2], replicated, may hold values from 0 to 129
- products: int32 [218, 2], replicated, may hold values from 0 to 129
- yields: float32 [218, 2], replicated, may hold values from 0.2 to 0.5
- reaction_index: int32 [64], P('pgrp'), may hold values from 0 to 217
Outputs:
- concentrations_out: float32 [130, 16, 256], P(None, 'tile')
- tangents_out: float32 [64, 130, 16, 256], P('pgrp', None, 'tile')
Inputs may be any that keep to these rules, and one draw needn't show every extreme that they name: `substeps`: each column needs at least one substep; some column has 4.
All inputs are finite; a program needn't handle non-finite values.
Results may differ from a plain program's by a relative error of at most 0.0003.
Values sent between devices are 32-bit elements; how exact they have to be, the bound alone decides.
No kernel may reach another device: no remote copies, remote signals or barrier semaphores. Data moves between devices by JAX's collectives and lax.ppermute only.
A program may use at most 256 MiB of HBM per device.

v0:
```python
import math

import jax
import jax.numpy as jnp
from jax import lax
from jax.sharding import PartitionSpec as P

CX = 16
CY = 16


def passed_along(value, axis, by):
    size = lax.axis_size(axis)
    pairs = [(i, i + by) for i in range(size) if 0 <= i + by < size]
    return lax.ppermute(value, axis, pairs)


def stoich(reactants, products, yields, species_count):
    species = lax.iota(jnp.int32, species_count)[:, None]
    uses_one = (species == reactants[:, 0][None, :]).astype(jnp.float32)
    uses_two = (species == reactants[:, 1][None, :]).astype(jnp.float32)
    produced = yields[:, 0][None, :] * (species == products[:, 0][None, :]).astype(jnp.float32)
    produced = produced + yields[:, 1][None, :] * (species == products[:, 1][None, :]).astype(
        jnp.float32
    )
    net_change = produced - uses_one - uses_two
    return (net_change, net_change * uses_one, net_change * uses_two)


def jacobian_apply(vector, reactant_one, reactant_two, rate_rows, reactants, net_change):
    along_one = jnp.take(vector, reactants[:, 0], axis=-2)
    along_two = jnp.take(vector, reactants[:, 1], axis=-2)
    mixed = rate_rows * (reactant_two * along_one + reactant_one * along_two)
    return jnp.einsum("sr,...rx->...sx", net_change, mixed, precision=lax.Precision.HIGHEST)


def relax(right, apply, factor, diagonal, divisor):
    result = right / divisor
    result = (right + factor * (apply(result) - diagonal * result)) / divisor
    return result


def prepare(conc, rate_rows, counts, index, reactants, net_one, net_two):
    active = index < counts
    factor = 1.0 / jnp.maximum(counts, 1).astype(jnp.float32)
    reactant_one = jnp.take(conc, reactants[:, 0], axis=0)
    reactant_two = jnp.take(conc, reactants[:, 1], axis=0)
    fluxes = rate_rows * reactant_one * reactant_two
    diagonal = jnp.dot(
        net_one, rate_rows * reactant_two, precision=lax.Precision.HIGHEST
    ) + jnp.dot(net_two, rate_rows * reactant_one, precision=lax.Precision.HIGHEST)
    return (active, factor, reactant_one, reactant_two, fluxes, diagonal, rate_rows)


def base_update(conc, state, reactants, net_change):
    active, factor, reactant_one, reactant_two, fluxes, diagonal, rate_rows = state
    divisor = 1.0 - factor * diagonal

    def apply(vector):
        return jacobian_apply(vector, reactant_one, reactant_two, rate_rows, reactants, net_change)

    right = factor * jnp.dot(net_change, fluxes, precision=lax.Precision.HIGHEST)
    return jnp.where(active, conc + relax(right, apply, factor, diagonal, divisor), conc)


def tangent_update(sens, state, reactants, net_change, columns, chosen):
    active, factor, reactant_one, reactant_two, fluxes, diagonal, rate_rows = state
    divisor = 1.0 - factor * diagonal

    def apply(vector):
        return jacobian_apply(vector, reactant_one, reactant_two, rate_rows, reactants, net_change)

    forcing = columns[:, :, None] * jnp.take(fluxes, chosen, axis=0)[:, None, :]
    right = factor * (apply(sens) + forcing)
    return jnp.where(active, sens + relax(right, apply, factor, diagonal, divisor), sens)


def advect(extended, courant_local, axis):
    length = extended.shape[axis] - 4

    def cut(offset):
        return lax.slice_in_dim(extended, offset, offset + length, axis=axis)

    minus_two, minus_one, centre, plus_one, plus_two = (cut(0), cut(1), cut(2), cut(3), cut(4))
    third = jnp.where(
        courant_local > 0,
        plus_one - 3.0 * centre + 3.0 * minus_one - minus_two,
        plus_two - 3.0 * plus_one + 3.0 * centre - minus_one,
    )
    return (
        centre
        - courant_local * (plus_one - minus_one) * 0.5
        + courant_local * courant_local * (plus_one - 2.0 * centre + minus_one) * 0.5
        + courant_local * (1.0 - courant_local * courant_local) / 6.0 * third
    )


def from_x(strip, offset):
    return passed_along(strip, "tile", offset)


def from_y(strip, offset):
    return passed_along(strip, "tile", offset)


def run_chemistry(
    conc, sens, rate_rows, counts, reactants, net_change, net_one, net_two, columns, chosen
):
    highest = jnp.max(counts)

    def own_turn(index, carry):
        whole, whole_sens = carry
        state = prepare(whole, rate_rows, counts, index, reactants, net_one, net_two)
        whole_sens = tangent_update(whole_sens, state, reactants, net_change, columns, chosen)
        whole = base_update(whole, state, reactants, net_change)
        return (whole, whole_sens)

    conc, sens = lax.fori_loop(0, highest, own_turn, (conc, sens))
    return (conc, sens)


def to_grid(conc, sens, rows_x, rows_y):
    stacked = jnp.concatenate([conc[None], sens], axis=0).reshape(-1, rows_x, rows_y)
    return stacked.transpose(1, 2, 0)


def per_device(
    concentrations, tangents, rates, substeps, courant, reactants, products, yields, reaction_index
):
    species_count = concentrations.shape[0]
    conc = concentrations[:, 0, :]
    sens = tangents[:, :, 0, :]
    group = sens.shape[0]
    rate_rows = rates[:, 0, :]
    counts = substeps[0]
    net_change, net_one, net_two = stoich(reactants, products, yields, species_count)
    columns = jnp.take(net_change, reaction_index, axis=1).T
    across = math.isqrt(lax.axis_size("tile"))
    conc, sens = run_chemistry(
        conc,
        sens,
        rate_rows,
        counts,
        reactants,
        net_change,
        net_one,
        net_two,
        columns,
        reaction_index,
    )
    field = to_grid(conc, sens, CX, CY)
    courant_x = courant[0, 0].reshape(CX, CY)[:, :, None]
    courant_y = courant[1, 0].reshape(CX, CY)[:, :, None]
    western = from_x(field[CX - 2 :], across)
    eastern = from_x(field[:2], -across)
    extended = jnp.concatenate([western, field, eastern], axis=0)
    moved = advect(extended, courant_x, 0)
    southern = from_y(moved[:, CY - 2 :], 1)
    northern = from_y(moved[:, :2], -1)
    final = advect(jnp.concatenate([southern, moved, northern], axis=1), courant_y, 1)
    result = final.transpose(2, 0, 1).reshape(group + 1, species_count, CX * CY)
    conc_out = result[0].reshape(species_count, 1, CX * CY)
    sens_out = result[1:].reshape(group, species_count, 1, CX * CY)
    return (conc_out, sens_out)


def solution(mesh):
    in_specs = (
        P(None, "tile", None),
        P("pgrp", None, "tile", None),
        P(None, "tile", None),
        P("tile", None),
        P(None, "tile", None),
        P(),
        P(),
        P(),
        P("pgrp"),
    )
    out_specs = (P(None, "tile", None), P("pgrp", None, "tile", None))
    return jax.shard_map(
        per_device, mesh=mesh, in_specs=in_specs, out_specs=out_specs, check_vma=False
    )
```

profile of v0, /device:TPU:13, one launch (start us, length us, event | category | flops | bytes accessed | tf_op | source)
XLA Modules:
  0.0 465.4 jit_solution(9148428094091939670)
XLA Ops:
  2.0 1.0 copy.52
  3.0 4.8 %copy.51 = f32[32,130,1,256]{3,1,0,2:T(8,128)} copy(f32[32,130,1,256]{3,2,1,0:T(1,128)} %param.18) | data formatting | bytes 8519680 | tf_op jit(solution)/shard_map/squeeze | solution.py:132
  9.5 340.3 %while.14 = (s32[]{:T(128)}, f32[130,256]{1,0:T(8,128)S(1)}, f32[32,130,256]{2,1,0:T(8,128)}, s32[]{:T(128)}, s32[256]{0:T(256)S(1)}, /*index=5*/s32[218,2]{0,1:...) while((s32[]{:T(128)}, f32[130,256]{1,0:T(8,128)S(1)}, ...), condition=%wide.region_2.6_spmd.clone.clone, body=%wide.region_1.5_spmd.clone.clone.sunk | while | flops 5960630272 | bytes 191905776 | solution.py:118
  16.3 5.7 %copy.60 = f32[32,130,256]{2,0,1:T(8,128)} copy(f32[32,130,256]{2,1,0:T(8,128)} %get-tuple-element.453) | data formatting | bytes 8519680 | tf_op jit(solution)/shard_map/while
  22.0 6.1 %gather_fusion.5 = f32[218,32,256]{2,1,0:T(8,128)} fusion(f32[32,130,256]{2,0,1:T(8,128)} %copy.60, s32[1024]{0:T(1024)S(1)} %pad_clamp_fusion.8), kind=kCustom, calls=%fused_computation.5.clone.clone.1 | custom fusion | bytes 14287720 | tf_op jit(solution)/shard_map/while/body/jit(_take)/gather | solution.py:32
  28.1 6.2 %gather_fusion.6 = f32[218,32,256]{2,1,0:T(8,128)} fusion(f32[32,130,256]{2,0,1:T(8,128)} %copy.60, s32[1024]{0:T(1024)S(1)} %pad_clamp_fusion.7), kind=kCustom, calls=%fused_computation.2.clone.clone.1 | custom fusion | bytes 14287720 | tf_op jit(solution)/shard_map/while/body/jit(_take)/gather | solution.py:31
  34.3 6.1 %fusion.145 = f32[32,218,256]{2,0,1:T(8,128)S(1)} fusion(f32[218,32,256]{2,1,0:T(8,128)} %gather_fusion.5, f32[218,32,256]{2,1,0:T(8,128)} %gather_fusion.6, f32[218,256]{1,0:T(8,128)S(1)} %get-tuple-element.427, f32[218,256]{1,0:T(8,128)S(1)} %get-tuple-element.428, f32[218,256]{1,0:T(8,128)S(1)} %bitcast.142, ...), kind=kLoop, calls=%fused_computation.23.clone.1 | loop fusion | flops 10715136 | bytes 22100404 | tf_op jit(solution)/shard_map/while/body/mul | solution.py:33
  40.4 14.2 %fusion.146 = (f32[32,130,256]{2,1,0:T(8,128)S(1)}, f32[32,256,130]{1,2,0:T(8,128)}) fusion(f32[130,256]{1,0:T(8,128)S(1)} %get-tuple-element.431, f32[32,256]{1,0:T(8,128)S(1)} %broadcast_select_fusion.7, f32[32,130]{1,0:T(8,128)S(1)} %get-tuple-element.476, f32[256]{0:T(256)S(1)} %convert_divide_fusion.2, s32[218]{0:T(256)S(1)} %get-tuple-element.483, ...), kind=kOutput, calls=%fused_computation.32.clone.2 | convolution fusion | flops 2790507008 | bytes 15851888 | tf_op jit(solution)/shard_map/while/body/sr,...rx->...sx/dot_general | solution.py:34
  54.6 3.3 copy.61
  58.0 6.1 %gather_fusion.7 = f32[218,32,256]{2,1,0:T(8,128)} fusion(f32[32,130,256]{2,0,1:T(8,128)} %copy.61, s32[1024]{0:T(1024)S(1)} %pad_clamp_fusion.8), kind=kCustom, calls=%fused_computation.7.clone.clone.1 | custom fusion | bytes 14287720 | tf_op jit(solution)/shard_map/while/body/jit(_take)/gather | solution.py:32
  64.1 6.2 %gather_fusion.8 = f32[218,32,256]{2,1,0:T(8,128)} fusion(f32[32,130,256]{2,0,1:T(8,128)} %copy.61, s32[1024]{0:T(1024)S(1)} %pad_clamp_fusion.7), kind=kCustom, calls=%fused_computation.6.clone.clone.1 | custom fusion | bytes 14287720 | tf_op jit(solution)/shard_map/while/body/jit(_take)/gather | solution.py:31
  70.3 6.3 %fusion.147 = f32[32,218,256]{2,0,1:T(8,128)S(1)} fusion(f32[218,32,256]{2,1,0:T(8,128)} %gather_fusion.7, f32[218,32,256]{2,1,0:T(8,128)} %gather_fusion.8, f32[218,256]{1,0:T(8,128)S(1)} %get-tuple-element.427, f32[218,256]{1,0:T(8,128)S(1)} %get-tuple-element.428, f32[218,256]{1,0:T(8,128)S(1)} %bitcast.143, ...), kind=kLoop, calls=%fused_computation.19.clone.1 | loop fusion | flops 10715136 | bytes 22100404 | tf_op jit(solution)/shard_map/while/body/mul | solution.py:33
  76.6 15.6 %add_select_fusion.2 = f32[32,130,256]{2,1,0:T(8,128)S(1)} fusion(f32[32,130,256]{2,1,0:T(8,128)S(1)} %bitcast.136, f32[32,256,130]{1,2,0:T(8,128)} %get-tuple-element.432, f32[130,256]{1,0:T(8,128)S(1)} %get-tuple-element.430, f32[130,256]{1,0:T(8,128)S(1)} %get-tuple-element.431, f32[32,256]{1,0:T(8,128)S(1)} %broadcast_select_fusion.7, ...), kind=kOutput, calls=%fused_computation.25.clone.1 | convolution fusion | flops 2797961728 | bytes 20245104 | tf_op jit(solution)/shard_map/while/body/sr,...rx->...sx/dot_general | solution.py:34
  92.3 2.1 copy-done
  101.2 5.7 %copy.60 = f32[32,130,256]{2,0,1:T(8,128)} copy(f32[32,130,256]{2,1,0:T(8,128)} %get-tuple-element.453) | data formatting | bytes 8519680 | tf_op jit(solution)/shard_map/while
  106.9 6.1 %gather_fusion.5 = f32[218,32,256]{2,1,0:T(8,128)} fusion(f32[32,130,256]{2,0,1:T(8,128)} %copy.60, s32[1024]{0:T(1024)S(1)} %pad_clamp_fusion.8), kind=kCustom, calls=%fused_computation.5.clone.clone.1 | custom fusion | bytes 14287720 | tf_op jit(solution)/shard_map/while/body/jit(_take)/gather | solution.py:32
  113.0 6.2 %gather_fusion.6 = f32[218,32,256]{2,1,0:T(8,128)} fusion(f32[32,130,256]{2,0,1:T(8,128)} %copy.60, s32[1024]{0:T(1024)S(1)} %pad_clamp_fusion.7), kind=kCustom, calls=%fused_computation.2.clone.clone.1 | custom fusion | bytes 14287720 | tf_op jit(solution)/shard_map/while/body/jit(_take)/gather | solution.py:31
  119.2 6.1 %fusion.145 = f32[32,218,256]{2,0,1:T(8,128)S(1)} fusion(f32[218,32,256]{2,1,0:T(8,128)} %gather_fusion.5, f32[218,32,256]{2,1,0:T(8,128)} %gather_fusion.6, f32[218,256]{1,0:T(8,128)S(1)} %get-tuple-element.427, f32[218,256]{1,0:T(8,128)S(1)} %get-tuple-element.428, f32[218,256]{1,0:T(8,128)S(1)} %bitcast.142, ...), kind=kLoop, calls=%fused_computation.23.clone.1 | loop fusion | flops 10715136 | bytes 22100404 | tf_op jit(solution)/shard_map/while/body/mul | solution.py:33
  125.3 14.2 %fusion.146 = (f32[32,130,256]{2,1,0:T(8,128)S(1)}, f32[32,256,130]{1,2,0:T(8,128)}) fusion(f32[130,256]{1,0:T(8,128)S(1)} %get-tuple-element.431, f32[32,256]{1,0:T(8,128)S(1)} %broadcast_select_fusion.7, f32[32,130]{1,0:T(8,128)S(1)} %get-tuple-element.476, f32[256]{0:T(256)S(1)} %convert_divide_fusion.2, s32[218]{0:T(256)S(1)} %get-tuple-element.483, ...), kind=kOutput, calls=%fused_computation.32.clone.2 | convolution fusion | flops 2790507008 | bytes 15851888 | tf_op jit(solution)/shard_map/while/body/sr,...rx->...sx/dot_general | solution.py:34
  139.5 3.3 copy.61
  142.8 6.1 %gather_fusion.7 = f32[218,32,256]{2,1,0:T(8,128)} fusion(f32[32,130,256]{2,0,1:T(8,128)} %copy.61, s32[1024]{0:T(1024)S(1)} %pad_clamp_fusion.8), kind=kCustom, calls=%fused_computation.7.clone.clone.1 | custom fusion | bytes 14287720 | tf_op jit(solution)/shard_map/while/body/jit(_take)/gather | solution.py:32
  148.9 6.2 %gather_fusion.8 = f32[218,32,256]{2,1,0:T(8,128)} fusion(f32[32,130,256]{2,0,1:T(8,128)} %copy.61, s32[1024]{0:T(1024)S(1)} %pad_clamp_fusion.7), kind=kCustom, calls=%fused_computation.6.clone.clone.1 | custom fusion | bytes 14287720 | tf_op jit(solution)/shard_map/while/body/jit(_take)/gather | solution.py:31
  155.2 6.3 %fusion.147 = f32[32,218,256]{2,0,1:T(8,128)S(1)} fusion(f32[218,32,256]{2,1,0:T(8,128)} %gather_fusion.7, f32[218,32,256]{2,1,0:T(8,128)} %gather_fusion.8, f32[218,256]{1,0:T(8,128)S(1)} %get-tuple-element.427, f32[218,256]{1,0:T(8,128)S(1)} %get-tuple-element.428, f32[218,256]{1,0:T(8,128)S(1)} %bitcast.143, ...), kind=kLoop, calls=%fused_computation.19.clone.1 | loop fusion | flops 10715136 | bytes 22100404 | tf_op jit(solution)/shard_map/while/body/mul | solution.py:33
  161.5 15.6 %add_select_fusion.2 = f32[32,130,256]{2,1,0:T(8,128)S(1)} fusion(f32[32,130,256]{2,1,0:T(8,128)S(1)} %bitcast.136, f32[32,256,130]{1,2,0:T(8,128)} %get-tuple-element.432, f32[130,256]{1,0:T(8,128)S(1)} %get-tuple-element.430, f32[130,256]{1,0:T(8,128)S(1)} %get-tuple-element.431, f32[32,256]{1,0:T(8,128)S(1)} %broadcast_select_fusion.7, ...), kind=kOutput, calls=%fused_computation.25.clone.1 | convolution fusion | flops 2797961728 | bytes 20245104 | tf_op jit(solution)/shard_map/while/body/sr,...rx->...sx/dot_general | solution.py:34
  177.1 2.1 copy-done
  186.1 5.7 %copy.60 = f32[32,130,256]{2,0,1:T(8,128)} copy(f32[32,130,256]{2,1,0:T(8,128)} %get-tuple-element.453) | data formatting | bytes 8519680 | tf_op jit(solution)/shard_map/while
  191.7 6.1 %gather_fusion.5 = f32[218,32,256]{2,1,0:T(8,128)} fusion(f32[32,130,256]{2,0,1:T(8,128)} %copy.60, s32[1024]{0:T(1024)S(1)} %pad_clamp_fusion.8), kind=kCustom, calls=%fused_computation.5.clone.clone.1 | custom fusion | bytes 14287720 | tf_op jit(solution)/shard_map/while/body/jit(_take)/gather | solution.py:32
  197.8 6.2 %gather_fusion.6 = f32[218,32,256]{2,1,0:T(8,128)} fusion(f32[32,130,256]{2,0,1:T(8,128)} %copy.60, s32[1024]{0:T(1024)S(1)} %pad_clamp_fusion.7), kind=kCustom, calls=%fused_computation.2.clone.clone.1 | custom fusion | bytes 14287720 | tf_op jit(solution)/shard_map/while/body/jit(_take)/gather | solution.py:31
  204.0 6.1 %fusion.145 = f32[32,218,256]{2,0,1:T(8,128)S(1)} fusion(f32[218,32,256]{2,1,0:T(8,128)} %gather_fusion.5, f32[218,32,256]{2,1,0:T(8,128)} %gather_fusion.6, f32[218,256]{1,0:T(8,128)S(1)} %get-tuple-element.427, f32[218,256]{1,0:T(8,128)S(1)} %get-tuple-element.428, f32[218,256]{1,0:T(8,128)S(1)} %bitcast.142, ...), kind=kLoop, calls=%fused_computation.23.clone.1 | loop fusion | flops 10715136 | bytes 22100404 | tf_op jit(solution)/shard_map/while/body/mul | solution.py:33
  210.2 14.2 %fusion.146 = (f32[32,130,256]{2,1,0:T(8,128)S(1)}, f32[32,256,130]{1,2,0:T(8,128)}) fusion(f32[130,256]{1,0:T(8,128)S(1)} %get-tuple-element.431, f32[32,256]{1,0:T(8,128)S(1)} %broadcast_select_fusion.7, f32[32,130]{1,0:T(8,128)S(1)} %get-tuple-element.476, f32[256]{0:T(256)S(1)} %convert_divide_fusion.2, s32[218]{0:T(256)S(1)} %get-tuple-element.483, ...), kind=kOutput, calls=%fused_computation.32.clone.2 | convolution fusion | flops 2790507008 | bytes 15851888 | tf_op jit(solution)/shard_map/while/body/sr,...rx->...sx/dot_general | solution.py:34
  224.4 3.3 copy.61
  227.7 6.1 %gather_fusion.7 = f32[218,32,256]{2,1,0:T(8,128)} fusion(f32[32,130,256]{2,0,1:T(8,128)} %copy.61, s32[1024]{0:T(1024)S(1)} %pad_clamp_fusion.8), kind=kCustom, calls=%fused_computation.7.clone.clone.1 | custom fusion | bytes 14287720 | tf_op jit(solution)/shard_map/while/body/jit(_take)/gather | solution.py:32
  233.8 6.2 %gather_fusion.8 = f32[218,32,256]{2,1,0:T(8,128)} fusion(f32[32,130,256]{2,0,1:T(8,128)} %copy.61, s32[1024]{0:T(1024)S(1)} %pad_clamp_fusion.7), kind=kCustom, calls=%fused_computation.6.clone.clone.1 | custom fusion | bytes 14287720 | tf_op jit(solution)/shard_map/while/body/jit(_take)/gather | solution.py:31
  240.0 6.3 %fusion.147 = f32[32,218,256]{2,0,1:T(8,128)S(1)} fusion(f32[218,32,256]{2,1,0:T(8,128)} %gather_fusion.7, f32[218,32,256]{2,1,0:T(8,128)} %gather_fusion.8, f32[218,256]{1,0:T(8,128)S(1)} %get-tuple-element.427, f32[218,256]{1,0:T(8,128)S(1)} %get-tuple-element.428, f32[218,256]{1,0:T(8,128)S(1)} %bitcast.143, ...), kind=kLoop, calls=%fused_computation.19.clone.1 | loop fusion | flops 10715136 | bytes 22100404 | tf_op jit(solution)/shard_map/while/body/mul | solution.py:33
  246.4 15.6 %add_select_fusion.2 = f32[32,130,256]{2,1,0:T(8,128)S(1)} fusion(f32[32,130,256]{2,1,0:T(8,128)S(1)} %bitcast.136, f32[32,256,130]{1,2,0:T(8,128)} %get-tuple-element.432, f32[130,256]{1,0:T(8,128)S(1)} %get-tuple-element.430, f32[130,256]{1,0:T(8,128)S(1)} %get-tuple-element.431, f32[32,256]{1,0:T(8,128)S(1)} %broadcast_select_fusion.7, ...), kind=kOutput, calls=%fused_computation.25.clone.1 | convolution fusion | flops 2797961728 | bytes 20245104 | tf_op jit(solution)/shard_map/while/body/sr,...rx->...sx/dot_general | solution.py:34
  262.0 2.1 copy-done
  270.9 5.7 %copy.60 = f32[32,130,256]{2,0,1:T(8,128)} copy(f32[32,130,256]{2,1,0:T(8,128)} %get-tuple-element.453) | data formatting | bytes 8519680 | tf_op jit(solution)/shard_map/while
  276.6 6.1 %gather_fusion.5 = f32[218,32,256]{2,1,0:T(8,128)} fusion(f32[32,130,256]{2,0,1:T(8,128)} %copy.60, s32[1024]{0:T(1024)S(1)} %pad_clamp_fusion.8), kind=kCustom, calls=%fused_computation.5.clone.clone.1 | custom fusion | bytes 14287720 | tf_op jit(solution)/shard_map/while/body/jit(_take)/gather | solution.py:32
  282.7 6.2 %gather_fusion.6 = f32[218,32,256]{2,1,0:T(8,128)} fusion(f32[32,130,256]{2,0,1:T(8,128)} %copy.60, s32[1024]{0:T(1024)S(1)} %pad_clamp_fusion.7), kind=kCustom, calls=%fused_computation.2.clone.clone.1 | custom fusion | bytes 14287720 | tf_op jit(solution)/shard_map/while/body/jit(_take)/gather | solution.py:31
  288.9 6.1 %fusion.145 = f32[32,218,256]{2,0,1:T(8,128)S(1)} fusion(f32[218,32,256]{2,1,0:T(8,128)} %gather_fusion.5, f32[218,32,256]{2,1,0:T(8,128)} %gather_fusion.6, f32[218,256]{1,0:T(8,128)S(1)} %get-tuple-element.427, f32[218,256]{1,0:T(8,128)S(1)} %get-tuple-element.428, f32[218,256]{1,0:T(8,128)S(1)} %bitcast.142, ...), kind=kLoop, calls=%fused_computation.23.clone.1 | loop fusion | flops 10715136 | bytes 22100404 | tf_op jit(solution)/shard_map/while/body/mul | solution.py:33
  295.0 14.2 %fusion.146 = (f32[32,130,256]{2,1,0:T(8,128)S(1)}, f32[32,256,130]{1,2,0:T(8,128)}) fusion(f32[130,256]{1,0:T(8,128)S(1)} %get-tuple-element.431, f32[32,256]{1,0:T(8,128)S(1)} %broadcast_select_fusion.7, f32[32,130]{1,0:T(8,128)S(1)} %get-tuple-element.476, f32[256]{0:T(256)S(1)} %convert_divide_fusion.2, s32[218]{0:T(256)S(1)} %get-tuple-element.483, ...), kind=kOutput, calls=%fused_computation.32.clone.2 | convolution fusion | flops 2790507008 | bytes 15851888 | tf_op jit(solution)/shard_map/while/body/sr,...rx->...sx/dot_general | solution.py:34
  309.2 3.3 copy.61
  312.6 6.1 %gather_fusion.7 = f32[218,32,256]{2,1,0:T(8,128)} fusion(f32[32,130,256]{2,0,1:T(8,128)} %copy.61, s32[1024]{0:T(1024)S(1)} %pad_clamp_fusion.8), kind=kCustom, calls=%fused_computation.7.clone.clone.1 | custom fusion | bytes 14287720 | tf_op jit(solution)/shard_map/while/body/jit(_take)/gather | solution.py:32
  318.7 6.2 %gather_fusion.8 = f32[218,32,256]{2,1,0:T(8,128)} fusion(f32[32,130,256]{2,0,1:T(8,128)} %copy.61, s32[1024]{0:T(1024)S(1)} %pad_clamp_fusion.7), kind=kCustom, calls=%fused_computation.6.clone.clone.1 | custom fusion | bytes 14287720 | tf_op jit(solution)/shard_map/while/body/jit(_take)/gather | solution.py:31
  324.9 6.3 %fusion.147 = f32[32,218,256]{2,0,1:T(8,128)S(1)} fusion(f32[218,32,256]{2,1,0:T(8,128)} %gather_fusion.7, f32[218,32,256]{2,1,0:T(8,128)} %gather_fusion.8, f32[218,256]{1,0:T(8,128)S(1)} %get-tuple-element.427, f32[218,256]{1,0:T(8,128)S(1)} %get-tuple-element.428, f32[218,256]{1,0:T(8,128)S(1)} %bitcast.143, ...), kind=kLoop, calls=%fused_computation.19.clone.1 | loop fusion | flops 10715136 | bytes 22100404 | tf_op jit(solution)/shard_map/while/body/mul | solution.py:33
  331.2 15.6 %add_select_fusion.2 = f32[32,130,256]{2,1,0:T(8,128)S(1)} fusion(f32[32,130,256]{2,1,0:T(8,128)S(1)} %bitcast.136, f32[32,256,130]{1,2,0:T(8,128)} %get-tuple-element.432, f32[130,256]{1,0:T(8,128)S(1)} %get-tuple-element.430, f32[130,256]{1,0:T(8,128)S(1)} %get-tuple-element.431, f32[32,256]{1,0:T(8,128)S(1)} %broadcast_select_fusion.7, ...), kind=kOutput, calls=%fused_computation.25.clone.1 | convolution fusion | flops 2797961728 | bytes 20245104 | tf_op jit(solution)/shard_map/while/body/sr,...rx->...sx/dot_general | solution.py:34
  346.9 2.1 copy-done
  349.8 4.8 %pad_maximum_fusion = f32[33,130,256]{2,1,0:T(8,128)} fusion(f32[32,130,256]{2,1,0:T(8,128)} %get-tuple-element.75, f32[1,130,256]{2,1,0:T(8,128)S(1)} %bitcast.133), kind=kLoop, calls=%fused_computation.139 | loop fusion | flops 1098240 | bytes 8785920 | tf_op jit(solution)/shard_map/concatenate | solution.py:123
  354.5 10.3 %copy.33 = f32[33,130,256]{1,0,2:T(8,128)} copy(f32[33,130,256]{2,1,0:T(8,128)} %pad_maximum_fusion) | data formatting | bytes 8785920 | tf_op jit(solution)/shard_map/concatenate | solution.py:123
  364.8 9.2 %reshape.147 = f32[4290,16,16]{0,2,1:T(8,128)} reshape(f32[33,130,256]{1,0,2:T(8,128)} %copy.33) | data formatting | bytes 8785920 | tf_op jit(solution)/shard_map/reshape | solution.py:123
  374.1 1.3 fusion.114
  375.4 1.9 collective-permute-start
  377.3 3.4 collective-permute-start.1
  380.8 10.0 %collective-permute-done = f32[2,16,4290]{2,1,0:T(8,128)S(1)} collective-permute-done((f32[2,16,4290]{2,1,0:T(8,128)S(1)}, f32[2,16,4290]{2,1,0:T(8,128)S(1)}, u32[]{:S(2)}, u32[]{:S(2)}) %collective-permute-start) | collective-permute-done | bytes 549152 | tf_op jit(solution)/shard_map/ppermute | solution.py:15
  390.8 1.9 collective-permute-done.1
  392.7 9.7 %fusion.110 = f32[16,16,4290]{2,1,0:T(8,128)S(1)} fusion(f32[2,16,4290]{2,1,0:T(8,128)S(1)} %collective-permute-done, f32[16,16,4290]{2,1,0:T(8,128)} %bitcast.146, f32[2,16,4290]{2,1,0:T(8,128)S(1)} %collective-permute-done.1, f32[16,16]{1,0:T(8,128)S(1)} %get-tuple-element.304, f32[16,16]{1,0:T(8,128)S(1)} %get-tuple-element.305, f32[16,16]{1,0:T(8,128)S(1)} %mul.294, ...), kind=kLoop, calls=%fused_computation.160 | loop fusion | flops 28554240 | bytes 9887488 | tf_op jit(solution)/shard_map/add | solution.py:91
  402.4 2.0 copy-done.1
  404.8 3.5 collective-permute-start.2
  408.3 2.1 collective-permute-start.3
  410.5 11.1 %collective-permute-done.2 = f32[16,2,4290]{2,1,0:T(2,128)S(1)} collective-permute-done((f32[16,2,4290]{2,1,0:T(2,128)S(1)}, f32[16,2,4290]{2,1,0:T(2,128)S(1)}, u32[]{:S(2)}, u32[]{:S(2)}) %collective-permute-start.2) | collective-permute-done | bytes 549152 | tf_op jit(solution)/shard_map/ppermute | solution.py:15
  422.1 13.8 %fusion.103 = f32[4290,16,16]{0,2,1:T(8,128)S(1)} fusion(f32[16,2,4290]{2,1,0:T(2,128)S(1)} %collective-permute-done.2, f32[16,16,4290]{2,1,0:T(8,128)} %copy-done.1, f32[16,2,4290]{2,1,0:T(2,128)S(1)} %collective-permute-done.3, f32[16,16]{1,0:T(8,128)S(1)} %get-tuple-element.302, f32[16,16]{1,0:T(8,128)S(1)} %get-tuple-element.303, ...), kind=kLoop, calls=%fused_computation.151 | loop fusion | flops 28554240 | bytes 9887488 | tf_op jit(solution)/shard_map/transpose | solution.py:161
  435.9 3.2 slice.147
  439.9 13.0 %reshape.148 = f32[32,130,1,256]{1,0,3,2:T(8,128)} reshape(f32[4160,16,16]{0,2,1:T(8,128)} %slice.147) | data formatting | bytes 8519680 | tf_op jit(solution)/shard_map/reshape | solution.py:163
  453.0 12.4 %copy.35 = f32[32,130,1,256]{3,2,1,0:T(1,128)} copy(f32[32,130,1,256]{1,0,3,2:T(8,128)} %reshape.148) | data formatting | bytes 8519680
  (149 shorter events, 29.3 us)
Async XLA Ops:
  2.0 5.8 %copy-start.2 = (f32[218,1,256]{2,1,0:T(1,128)S(1)}, f32[218,1,256]{2,1,0:T(1,128)}, u32[]{:S(2)}) copy-start(f32[218,1,256]{2,1,0:T(1,128)} %param.19) | copy-start | bytes 669700
  2.9 4.8 %copy-start.4 = (s32[218,2]{0,1:T(2,128)S(1)}, s32[218,2]{0,1:T(2,128)}, u32[]{:S(2)}) copy-start(s32[218,2]{0,1:T(2,128)} %param.22) | copy-start | bytes 5236
  2.9 4.8 %copy-start.5 = (f32[218,2]{0,1:T(2,128)S(1)}, f32[218,2]{0,1:T(2,128)}, u32[]{:S(2)}) copy-start(f32[218,2]{0,1:T(2,128)} %param.24) | copy-start | bytes 5236
  2.9 4.9 %copy-start.6 = (s32[218,2]{0,1:T(2,128)S(1)}, s32[218,2]{0,1:T(2,128)}, u32[]{:S(2)}) copy-start(s32[218,2]{0,1:T(2,128)} %param.23) | copy-start | bytes 5236
  2.9 4.9 %copy-start.3 = (s32[1,256]{1,0:T(1,128)S(1)}, s32[1,256]{1,0:T(1,128)}, u32[]{:S(2)}) copy-start(s32[1,256]{1,0:T(1,128)} %param.20) | copy-start | bytes 3076
  3.0 6.5 %copy-start.8 = (s32[32]{0:T(128)S(1)}, s32[32]{0:T(128)}, u32[]{:S(2)}) copy-start(s32[32]{0:T(128)} %param.25) | copy-start | bytes 388
  64.1 12.5 %slice-start = ((s8[4456448]{0:T(1024)(128)(4,1)}), s8[262144]{0:T(1024)(128)(4,1)S(1)}, s32[]{:S(2)}) async-start(s8[4456448]{0:T(1024)(128)(4,1)} %bitcast.135), calls=%async_computation | async-start | bytes 524288 | tf_op jit(solution)/shard_map/while
  70.3 6.3 %slice-start.1 = ((s8[4456448]{0:T(1024)(128)(4,1)}), s8[4194304]{0:T(1024)(128)(4,1)S(1)}, s32[]{:S(2)}) async-start(s8[4456448]{0:T(1024)(128)(4,1)} %bitcast.135), calls=%async_computation.1 | async-start | bytes 8388608 | tf_op jit(solution)/shard_map/while
  92.3 2.1 copy-start
  148.9 12.5 %slice-start = ((s8[4456448]{0:T(1024)(128)(4,1)}), s8[262144]{0:T(1024)(128)(4,1)S(1)}, s32[]{:S(2)}) async-start(s8[4456448]{0:T(1024)(128)(4,1)} %bitcast.135), calls=%async_computation | async-start | bytes 524288 | tf_op jit(solution)/shard_map/while
  155.2 6.3 %slice-start.1 = ((s8[4456448]{0:T(1024)(128)(4,1)}), s8[4194304]{0:T(1024)(128)(4,1)S(1)}, s32[]{:S(2)}) async-start(s8[4456448]{0:T(1024)(128)(4,1)} %bitcast.135), calls=%async_computation.1 | async-start | bytes 8388608 | tf_op jit(solution)/shard_map/while
  177.1 2.1 copy-start
  233.8 12.5 %slice-start = ((s8[4456448]{0:T(1024)(128)(4,1)}), s8[262144]{0:T(1024)(128)(4,1)S(1)}, s32[]{:S(2)}) async-start(s8[4456448]{0:T(1024)(128)(4,1)} %bitcast.135), calls=%async_computation | async-start | bytes 524288 | tf_op jit(solution)/shard_map/while
  240.0 6.3 %slice-start.1 = ((s8[4456448]{0:T(1024)(128)(4,1)}), s8[4194304]{0:T(1024)(128)(4,1)S(1)}, s32[]{:S(2)}) async-start(s8[4456448]{0:T(1024)(128)(4,1)} %bitcast.135), calls=%async_computation.1 | async-start | bytes 8388608 | tf_op jit(solution)/shard_map/while
  262.0 2.1 copy-start
  318.7 12.5 %slice-start = ((s8[4456448]{0:T(1024)(128)(4,1)}), s8[262144]{0:T(1024)(128)(4,1)S(1)}, s32[]{:S(2)}) async-start(s8[4456448]{0:T(1024)(128)(4,1)} %bitcast.135), calls=%async_computation | async-start | bytes 524288 | tf_op jit(solution)/shard_map/while
  324.9 6.3 %slice-start.1 = ((s8[4456448]{0:T(1024)(128)(4,1)}), s8[4194304]{0:T(1024)(128)(4,1)S(1)}, s32[]{:S(2)}) async-start(s8[4456448]{0:T(1024)(128)(4,1)} %bitcast.135), calls=%async_computation.1 | async-start | bytes 8388608 | tf_op jit(solution)/shard_map/while
  346.9 2.1 copy-start
  364.8 15.8 %copy-start.7 = (f32[2,1,256]{2,1,0:T(1,128)S(1)}, f32[2,1,256]{2,1,0:T(1,128)}, u32[]{:S(2)}) copy-start(f32[2,1,256]{2,1,0:T(1,128)} %param.21) | copy-start | bytes 6148
  375.4 15.4 %collective-permute-start = (f32[2,16,4290]{2,1,0:T(8,128)S(1)}, f32[2,16,4290]{2,1,0:T(8,128)S(1)}, u32[]{:S(2)}, u32[]{:S(2)}) collective-permute-start(f32[2,16,4290]{2,1,0:T(8,128)S(1)} %get-tuple-element.299), channel_id=1, source_target_pairs={{8,0},{10,2},{12,4},{14,6},{16,8},{18,10},{20,12},{22,14},{24,16},... | collective-permute-start | bytes 1647368 | tf_op jit(solution)/shard_map/ppermute | solution.py:15
  377.3 15.4 %collective-permute-start.1 = (f32[2,16,4290]{2,1,0:T(8,128)S(1)}, f32[2,16,4290]{2,1,0:T(8,128)S(1)}, u32[]{:S(2)}, u32[]{:S(2)}) collective-permute-start(f32[2,16,4290]{2,1,0:T(8,128)S(1)} %get-tuple-element.298), channel_id=1, source_target_pairs={{0,8},{2,10},{4,12},{6,14},{8,16},{10,18},{12,20},{14,22},{16,24},... | collective-permute-start | bytes 1647368 | tf_op jit(solution)/shard_map/ppermute | solution.py:15
  402.4 2.0 copy-start.1
  404.8 16.8 %collective-permute-start.2 = (f32[16,2,4290]{2,1,0:T(2,128)S(1)}, f32[16,2,4290]{2,1,0:T(2,128)S(1)}, u32[]{:S(2)}, u32[]{:S(2)}) collective-permute-start(f32[16,2,4290]{2,1,0:T(2,128)S(1)} %get-tuple-element.297), channel_id=1, source_target_pairs={{2,0},{4,2},{6,4},{8,6},{10,8},{12,10},{14,12},{16,14},{18,16},{20... | collective-permute-start | bytes 1647368 | tf_op jit(solution)/shard_map/ppermute | solution.py:15
  408.3 13.8 %collective-permute-start.3 = (f32[16,2,4290]{2,1,0:T(2,128)S(1)}, f32[16,2,4290]{2,1,0:T(2,128)S(1)}, u32[]{:S(2)}, u32[]{:S(2)}) collective-permute-start(f32[16,2,4290]{2,1,0:T(2,128)S(1)} %get-tuple-element.296), channel_id=1, source_target_pairs={{0,2},{2,4},{4,6},{6,8},{8,10},{10,12},{12,14},{14,16},{16,18},{18... | collective-permute-start | bytes 1647368 | tf_op jit(solution)/shard_map/ppermute | solution.py:15
where the time goes:
time: 468 us; the launch traced here: 465 us
  local copies, waits for them, and re-layouts  219 us (47%)
  matrix products  126 us (27%)
  other arithmetic  81.4 us (17%)
  waiting for transfers between devices  23.5 us (5%)
  starting transfers between devices  10.8 us (2%)
    dot_general x12, matrix products, jacobian_apply(): jnp.einsum('sr,...rx->...sx', net_change, mixed, precision=lax.Precision....  121 us
    gather x12, local copies, waits for them, and re-layouts, jacobian_apply(): along_one = jnp.take(vector, reactants[:, 0], axis=-2)  53.3 us
    gather x12, local copies, waits for them, and re-layouts, jacobian_apply(): along_two = jnp.take(vector, reactants[:, 1], axis=-2)  52.4 us
    mul x8, other arithmetic, jacobian_apply(): mixed = rate_rows * (reactant_two * along_one + reactant_one * along_two)  49.7 us
    while x28, local copies, waits for them, and re-layouts  31.1 us
    ppermute x4, waiting for transfers between devices, passed_along(): return lax.ppermute(value, axis, pairs)  23.5 us
    unnamed x20, local copies, waits for them, and re-layouts  16.2 us
    transpose x1, other arithmetic, per_device(): result = final.transpose(2, 0, 1).reshape(group + 1, species_count, CX * CY)  13.8 us
  transfers between devices with their start and end apart: 4, of which 4 were waited for; matrix products, arithmetic and copies ran while one was open for 0% of the time, Pallas kernels for 0%

commit v1 on v0

v1 whole, which is shorter than its diff:
```python
import functools
import math

import jax
import jax.numpy as jnp
import numpy as np
from jax import lax
from jax.experimental import pallas as pl
from jax.experimental.pallas import tpu as pltpu
from jax.sharding import PartitionSpec as P

CX = 16
CY = 16
NMAX = 4
LANES = 128
FAR = 99
UNROLL = 8
BUFFERS = 2
F32 = jnp.float32
BF16 = jnp.bfloat16


def orders():
    last, end = CX - 2, CY - 2
    west = [(i, j) for i in range(2) for j in range(CY)]
    east = [(i, j) for i in range(last, CX) for j in range(CY)]
    south = [(i, j) for j in range(2) for i in range(CX)]
    north = [(i, j) for j in range(end, CY) for i in range(CX)]
    strips = west + east + south + north
    edge = list(dict.fromkeys(strips))
    inner = [(i, j) for i in range(CX) for j in range(CY) if (i, j) not in set(edge)]
    order = edge + inner
    rows, columns = ((last, CX), (0, 2)), ((end, CY), (0, 2))
    corners = [
        [(i, j) for i in range(*rows[d // 2]) for j in range(*columns[d % 2])] for d in range(4)
    ]
    return order, strips, corners


def one_hot(source, wanted):
    place = {cell: k for k, cell in enumerate(source)}
    table = np.zeros((len(source), len(wanted)), np.float32)
    for lane, cell in enumerate(wanted):
        if cell is not None:
            table[place[cell], lane] = 1.0
    return table


def static_tables():
    order, strips, corners = orders()
    cells = [(i, j) for i in range(CX) for j in range(CY)]
    group = order[:LANES]
    permute = one_hot(cells, order)
    strip = one_hot(group, strips)
    corner = []
    for q in range(4):
        lanes = [None] * LANES
        for d in range(4):
            for c in range(4):
                lanes[d * 16 + q * 4 + c] = corners[d][c]
        corner.append(one_hot(group, lanes))
    place = {}
    for lane, cell in enumerate(strips):
        place.setdefault(cell, lane)
    conc_corner = np.zeros((4, LANES, LANES), np.float32)
    for d in range(4):
        for c in range(4):
            conc_corner[d, place[corners[d][c]], d * 16 + c] = 1.0
    entries = list(order)
    entries += [(i - CX, j) for i, j in strips[32:64]]
    entries += [(i + CX, j) for i, j in strips[0:32]]
    entries += [(i, j - CY) for i, j in strips[96:128]]
    entries += [(i, j + CY) for i, j in strips[64:96]]
    shift = ((-CX, -CY), (-CX, CY), (CX, -CY), (CX, CY))
    for d in range(4):
        for q in range(4):
            entries += [(i + shift[d][0], j + shift[d][1]) for i, j in corners[d]]
    entries += [(FAR, FAR)] * (4 * LANES - len(entries))
    middle = cells + [(i, j - CY) for i, j in strips[96:128]]
    middle += [(i, j + CY) for i, j in strips[64:96]]
    middle += [(-FAR, -FAR)] * (3 * LANES - len(middle))
    columns = np.array(entries, np.int32)
    mid_rows = np.array(middle, np.int32).T
    mid_columns = np.array(middle, np.int32)
    out_rows = np.array(cells, np.int32).T
    return {
        "permute": permute,
        "strip": strip,
        "corner": np.concatenate(corner, axis=0),
        "conc_corner": conc_corner.reshape(4 * LANES, LANES),
        "columns": columns,
        "mid_rows": mid_rows,
        "mid_columns": mid_columns,
        "out_rows": out_rows,
    }


def dot(left, right):
    return jnp.dot(left, right, preferred_element_type=F32)


def parts_of(value, count):
    parts = []
    for k in range(count):
        part = value.astype(BF16)
        parts.append(part)
        if k + 1 < count:
            value = value - part.astype(F32)
    return parts


def select_left(exact, value, count):
    return sum(dot(exact, part) for part in parts_of(value, count))


def select_right(value, exact, count):
    return sum(dot(part, exact) for part in parts_of(value, count))


def product(left_parts, value):
    high, low = parts_of(value, 2)
    return dot(left_parts[0], high) + (dot(left_parts[0], low) + dot(left_parts[1], high))


def product_right(value, right_parts):
    high, low = parts_of(value, 2)
    return dot(high, right_parts[0]) + (dot(low, right_parts[0]) + dot(high, right_parts[1]))


def lane_of(rows):
    return lax.broadcasted_iota(jnp.int32, (rows, LANES), 1)


def swap_blocks(arrays):
    lane = lane_of(arrays[0].shape[0])
    low = lane < 64
    even = (lane // 32) % 2 == 0
    a, b, c, d = arrays
    a, c = (
        jnp.where(low, a, pltpu.roll(c, 64, 1)),
        jnp.where(low, pltpu.roll(a, 64, 1), c),
    )
    b, d = (
        jnp.where(low, b, pltpu.roll(d, 64, 1)),
        jnp.where(low, pltpu.roll(b, 64, 1), d),
    )
    a, b = (
        jnp.where(even, a, pltpu.roll(b, 32, 1)),
        jnp.where(even, pltpu.roll(a, 96, 1), b),
    )
    c, d = (
        jnp.where(even, c, pltpu.roll(d, 32, 1)),
        jnp.where(even, pltpu.roll(c, 96, 1), d),
    )
    return [a, b, c, d]


def tangent_copies(source, target, sems):
    return [
        pltpu.make_async_copy(source.at[p], target.at[:, p // 8, :, p % 8, :], sems.at[p // 8])
        for p in range(source.shape[0])
    ]


def pick_columns(raw, table, target):
    species = raw.shape[0]
    for q in range(raw.shape[1]):
        both = jnp.concatenate(
            [
                raw[:, q, 0].reshape(species * 8, LANES),
                raw[:, q, 1].reshape(species * 8, LANES),
            ],
            axis=1,
        )
        picked = select_right(both, table[...], 2)
        target[0:species, q * 8 : (q + 1) * 8, :] = picked.reshape(species, 8, LANES)
    target[species] = jnp.zeros(target.shape[1:], F32)


def tangent_chemistry(
    ilist, ylist, chosen, a_ref, b_ref, flux_ref, fd_ref, fda_ref, h_ref, t, x, used, made, highest
):
    reactions = a_ref.shape[1]
    species = t.shape[0] - 1
    group = t.shape[1]
    zero = jnp.zeros(t.shape[1:], F32)
    sublane = lax.broadcasted_iota(jnp.int32, (8, LANES), 0)

    def clear(s, carry):
        for ref in used + made:
            ref[s] = zero
        return carry

    lax.fori_loop(0, species + 1, clear, 0)

    def apply(source, n):
        def body(step, carry):
            mixes = []
            for k in range(UNROLL):
                r = step * UNROLL + k
                mixes.append(
                    a_ref[n, pl.ds(r, 1), :] * source[ilist[r]]
                    + b_ref[n, pl.ds(r, 1), :] * source[ilist[reactions + r]]
                )
            for k in range(UNROLL):
                r = step * UNROLL + k
                i1, i2 = ilist[r], ilist[reactions + r]
                q1, q2 = ilist[2 * reactions + r], ilist[3 * reactions + r]
                lost, gained = used[k % BUFFERS], made[k % BUFFERS]
                mix = mixes[k]
                one, two = lost[i1], lost[i2]
                three, four = gained[q1], gained[q2]
                lost[i1] = one - mix
                lost[i2] = two - mix
                gained[q1] = three + ylist[r] * mix
                gained[q2] = four + ylist[reactions + r] * mix
            return carry

        lax.fori_loop(0, reactions // UNROLL, body, 0)

    def force(n):
        def body(p8, carry):
            at = sublane == p8
            for q in range(group // 8):
                r = chosen[q * 8 + p8]
                value = jnp.where(at, flux_ref[n, pl.ds(r, 1), :], 0.0)
                i1, i2 = ilist[r], ilist[reactions + r]
                q1, q2 = ilist[2 * reactions + r], ilist[3 * reactions + r]
                lost, gained = used[q % BUFFERS], made[q % BUFFERS]
                rows = slice(q * 8, (q + 1) * 8)
                one, two = lost[i1, rows, :], lost[i2, rows, :]
                three, four = gained[q1, rows, :], gained[q2, rows, :]
                lost[i1, rows, :] = one - value
                lost[i2, rows, :] = two - value
                gained[q1, rows, :] = three + ylist[r] * value
                gained[q2, rows, :] = four + ylist[reactions + r] * value
            return carry

        lax.fori_loop(0, 8, body, 0)

    def total(s):
        value = used[0][s] + made[0][s]
        for k in range(1, BUFFERS):
            value = value + (used[k][s] + made[k][s])
        return value

    def substep(n, carry):
        force(n)
        apply(t, n)

        def first(s, inner):
            right = total(s)
            start = right * fd_ref[n, pl.ds(s, 1), :]
            x[s] = start
            used[0][s] = start * h_ref[n, pl.ds(s, 1), :]
            for ref in used[1:] + made:
                ref[s] = zero
            return inner

        lax.fori_loop(0, species, first, 0, unroll=2)
        apply(x, n)

        def second(s, inner):
            t[s] = t[s] + total(s) * fda_ref[n, pl.ds(s, 1), :]
            for ref in used + made:
                ref[s] = zero
            return inner

        lax.fori_loop(0, species, second, 0, unroll=2)
        return carry

    x[species] = zero
    lax.fori_loop(0, highest, substep, 0)


def edge_kernel(
    ilist, ylist, chosen,
    conc, rates, counts, rrows, rcolumns, yrows, permute, strip, corner, tangents,
    t_out, conc_out, counts_out, a_b, b_b, flux_b, fd_b, fda_b, h_b,
    s0, s1, s2, s3, d0, d1, d2, d3,
    raw, t, x, a_a, b_a, flux_a, fd_a, fda_a, h_a, fold, net_parts, hot, base, *rest,
):
    sems = rest[-1]
    used, made = list(rest[:BUFFERS]), list(rest[BUFFERS : 2 * BUFFERS])
    species = conc.shape[0]
    reactions = a_a.shape[1]
    copies = tangent_copies(tangents, raw, sems)
    for copy in copies:
        copy.start()

    row = lax.broadcasted_iota(jnp.int32, (species, reactions), 0)
    uses_one = row == rrows[0:1, :]
    uses_two = row == rrows[1:2, :]
    net = (
        jnp.where(row == rrows[2:3, :], yrows[0:1, :], 0.0)
        + jnp.where(row == rrows[3:4, :], yrows[1:2, :], 0.0)
        - jnp.where(uses_one, 1.0, 0.0)
        - jnp.where(uses_two, 1.0, 0.0)
    )
    for k, value in enumerate((net, jnp.where(uses_one, net, 0.0), jnp.where(uses_two, net, 0.0))):
        high, low = parts_of(value, 2)
        net_parts[2 * k] = high
        net_parts[2 * k + 1] = low
    lane = lax.broadcasted_iota(jnp.int32, (reactions, species), 1)
    hot[0:reactions] = jnp.where(lane == rcolumns[:, 0:1], 1.0, 0.0).astype(BF16)
    hot[reactions:] = jnp.where(lane == rcolumns[:, 1:2], 1.0, 0.0).astype(BF16)
    same = rcolumns[:, 0:1] == rcolumns[:, 1:2]

    order = permute[...]
    base[...] = select_right(conc[...], order, 3)
    rate = select_right(rates[...], order, 3)
    count = dot(jnp.broadcast_to(counts[...].astype(F32), (8, counts.shape[1])).astype(BF16), order)
    counts_out[...] = count
    count = count[0:1, :]
    factor = 1.0 / count
    highest = jnp.max(count).astype(jnp.int32)

    def keep(n, value, ref_a, ref_b):
        ref_a[n] = value[:, :LANES]
        ref_b[n] = value[:, LANES:]

    def substep(n, carry):
        c = base[...]
        picked = select_left(hot[...], c, 3)
        one, two = picked[:reactions], picked[reactions:]
        a = rate * two
        b = rate * one
        flux = a * one
        nets = (net_parts[0], net_parts[1])
        diagonal = product((net_parts[2], net_parts[3]), a) + product(
            (net_parts[4], net_parts[5]), b
        )
        change = product(nets, flux)
        divisor = 1.0 - factor * diagonal
        fd = factor / divisor
        start = fd * change
        along = select_left(hot[...], start, 2)
        again = product(nets, a * along[:reactions] + b * along[reactions:])
        move = fd * (change + (again - diagonal * start))
        active = n.astype(F32) < count
        base[...] = c + jnp.where(active, move, 0.0)
        keep(n, jnp.where(same, 2.0 * (a + b), a), a_a, a_b)
        keep(n, jnp.where(same, 0.0, b), b_a, b_b)
        keep(n, jnp.where(same, 2.0 * flux, flux), flux_a, flux_b)
        keep(n, fd, fd_a, fd_b)
        keep(n, jnp.where(active, fd, 0.0), fda_a, fda_b)
        keep(n, count - 2.0 * diagonal, h_a, h_b)
        return carry

    lax.fori_loop(0, highest, substep, 0)
    conc_out[...] = base[...]

    for copy in copies:
        copy.wait()
    pick_columns(raw, permute.at[:, 0:LANES], t)
    own = jnp.max(count[:, :LANES]).astype(jnp.int32)
    tangent_chemistry(
        ilist, ylist, chosen, a_a, b_a, flux_a, fd_a, fda_a, h_a, t, x, used, made, own
    )
    t_out[...] = t[0:species]

    rows = species * 8
    blocks = [t[0:species, q * 8 : (q + 1) * 8, :].reshape(rows, LANES) for q in range(4)]
    strips = swap_blocks([select_right(block, strip[...], 2) for block in blocks])
    base_strips = select_right(base[:, 0:LANES], strip[...], 3)
    for ref, value in zip((s0, s1, s2, s3), strips, strict=True):
        ref[0:rows] = value
        ref[rows : rows + species] = base_strips
        ref[rows + species :] = jnp.zeros((ref.shape[0] - rows - species, LANES), F32)
    points = select_right(jnp.concatenate(blocks, axis=1), corner[...], 2)
    short = fold.shape[0] // 8
    fold[0:species] = points.reshape(species, 8, LANES)
    fold[species:] = jnp.zeros((fold.shape[0] - species, 8, LANES), F32)
    place = lane_of(short * 8) // 16
    for d, ref in enumerate((d0, d1, d2, d3)):
        value = jnp.zeros((short * 8, LANES), F32)
        for g in range(8):
            piece = fold[g * short : (g + 1) * short].reshape(short * 8, LANES)
            by = (16 * (g - d)) % LANES
            value = jnp.where(place == g, pltpu.roll(piece, by, 1) if by else piece, value)
        ref[0 : short * 8] = value
        ref[short * 8 : short * 8 + species] = base_strips
        ref[short * 8 + species :] = jnp.zeros(
            (ref.shape[0] - short * 8 - species, LANES), F32
        )


def inner_kernel(
    ilist, ylist, chosen,
    counts, a_b, b_b, flux_b, fd_b, fda_b, h_b, permute, tangents,
    t_out,
    raw, t, x, *rest,
):
    sems = rest[-1]
    used, made = list(rest[:BUFFERS]), list(rest[BUFFERS : 2 * BUFFERS])
    copies = tangent_copies(tangents, raw, sems)
    for copy in copies:
        copy.start()
    own = jnp.max(counts[0:1, LANES:]).astype(jnp.int32)
    for copy in copies:
        copy.wait()
    pick_columns(raw, permute.at[:, LANES:], t)
    tangent_chemistry(
        ilist, ylist, chosen, a_b, b_b, flux_b, fd_b, fda_b, h_b, t, x, used, made, own
    )
    t_out[...] = t[0 : t_out.shape[0]]


def weights(c):
    g = c * (1.0 - c * c) / 6.0
    up = c > 0
    half, square = 0.5 * c, 0.5 * c * c
    return (
        jnp.where(up, -g, 0.0),
        half + square + jnp.where(up, 3.0 * g, -g),
        1.0 - c * c + jnp.where(up, -3.0 * g, 3.0 * g),
        square - half + jnp.where(up, g, -3.0 * g),
        jnp.where(up, 0.0, g),
    )


def advect_kernel(
    t_a, t_b, conc, h0, h1, h2, h3, d0, d1, d2, d3, cx, cy,
    columns, mid_rows, mid_columns, out_rows, conc_corner,
    t_out, conc_out,
    done, unfold, w_parts, sem,
):
    species = conc.shape[0]
    rows = species * 8
    di = columns[:, 0:1] - mid_rows[0:1, :]
    dj = columns[:, 1:2] - mid_rows[1:2, :]
    first = jnp.zeros(di.shape, F32)
    for k, weight in enumerate(weights(cx[...])):
        first = jnp.where((di == k - 2) & (dj == 0), weight, first)
    di = mid_columns[:, 0:1] - out_rows[0:1, :]
    dj = mid_columns[:, 1:2] - out_rows[1:2, :]
    second = jnp.zeros(di.shape, F32)
    for k, weight in enumerate(weights(cy[...])):
        second = jnp.where((dj == k - 2) & (di == 0), weight, second)
    whole = jnp.dot(first, second, precision=lax.Precision.HIGHEST, preferred_element_type=F32)
    high, low = parts_of(whole, 2)
    w_parts[0] = high
    w_parts[1] = low

    halo = 2 * LANES
    line = lax.broadcasted_iota(jnp.int32, (LANES, halo), 0)

    def halo_weights(q):
        mask = (line // 4) % 4 == q
        return [
            jnp.concatenate(
                [
                    w_parts[k, halo : halo + LANES, :],
                    jnp.where(mask, w_parts[k, halo + LANES :, :], jnp.zeros((), BF16)),
                ],
                axis=0,
            )
            for k in range(2)
        ]

    local = [w_parts[k, 0:halo, :] for k in range(2)]

    short = unfold.shape[0] // 8
    place = lane_of(short * 8) // 16
    for g in range(8):
        value = jnp.zeros((short * 8, LANES), F32)
        for d, ref in enumerate((d0, d1, d2, d3)):
            piece = ref[0 : short * 8]
            by = (16 * (d - g)) % LANES
            value = jnp.where(place == d, pltpu.roll(piece, by, 1) if by else piece, value)
        unfold[g * short : (g + 1) * short] = value.reshape(short, 8, LANES)
    strips = swap_blocks([ref[0:rows] for ref in (h0, h1, h2, h3)])
    points = unfold[0:species].reshape(rows, LANES)
    copies = []
    for q in range(4):
        part = slice(q * 8, (q + 1) * 8)
        own = jnp.concatenate(
            [t_a[:, part, :].reshape(rows, LANES), t_b[:, part, :].reshape(rows, LANES)], axis=1
        )
        outer = jnp.concatenate([strips[q], points], axis=1)
        value = product_right(own, local) + product_right(outer, halo_weights(q))
        done[:, q, 0] = value[:, :LANES].reshape(species, 8, LANES)
        done[:, q, 1] = value[:, LANES:].reshape(species, 8, LANES)
        for p8 in range(8):
            copy = pltpu.make_async_copy(
                done.at[:, q, :, p8, :], t_out.at[q * 8 + p8], sem
            )
            copy.start()
            copies.append(copy)

    lane = lane_of(species)
    w, e, s, n = [ref[rows : rows + species] for ref in (h0, h1, h2, h3)]
    sides = jnp.where(
        lane < 64,
        jnp.where(lane < 32, pltpu.roll(w, 96, 1), pltpu.roll(e, 32, 1)),
        jnp.where(lane < 96, pltpu.roll(s, 96, 1), pltpu.roll(n, 32, 1)),
    )
    tips = jnp.zeros((species, LANES), F32)
    for d, ref in enumerate((d0, d1, d2, d3)):
        tips = tips + select_right(
            ref[short * 8 : short * 8 + species],
            conc_corner[d * LANES : (d + 1) * LANES, :],
            2,
        )
    conc_out[...] = product_right(conc[...], local) + product_right(
        jnp.concatenate([sides, tips], axis=1), halo_weights(0)
    )
    for copy in copies:
        copy.wait()


def passed_along(value, axis, by):
    size = lax.axis_size(axis)
    pairs = [(i, i + by) for i in range(size) if 0 <= i + by < size]
    return lax.ppermute(value, axis, pairs)


def padded(value, length, fill):
    return jnp.pad(value, (0, length - value.shape[0]), constant_values=fill)


def per_device(
    concentrations, tangents, rates, substeps, courant, reactants, products, yields, reaction_index
):
    species = concentrations.shape[0]
    cells = CX * CY
    group = tangents.shape[0]
    real = rates.shape[0]
    reactions = -(-real // UNROLL) * UNROLL
    across = math.isqrt(lax.axis_size("tile"))
    table = static_tables()
    vmem = pl.BlockSpec(memory_space=pltpu.VMEM)
    smem = pl.BlockSpec(memory_space=pltpu.SMEM)
    hbm = pl.BlockSpec(memory_space=pl.ANY)
    limit = pltpu.CompilerParams(vmem_limit_bytes=60 * 2**20)

    def shape(*sizes, dtype=F32):
        return jax.ShapeDtypeStruct(sizes, dtype)

    grid = courant[0, 0].reshape(CX, CY)
    south = passed_along(grid[:, CY - 2 :].T.reshape(1, 2 * CX), "tile", 1)
    north = passed_along(grid[:, :2].T.reshape(1, 2 * CX), "tile", -1)
    cx = jnp.concatenate(
        [courant[0], south, north, jnp.zeros((1, 3 * LANES - cells - 4 * CX), F32)], axis=1
    )

    r0, r1, p0, p1 = reactants[:, 0], reactants[:, 1], products[:, 0], products[:, 1]
    same, equal = r0 == r1, p0 == p1
    scale = jnp.where(same, 0.5, 1.0)
    ilist = jnp.concatenate(
        [
            padded(v, reactions, species)
            for v in (r0, jnp.where(same, species, r1), p0, jnp.where(equal, species, p1))
        ]
    )
    ylist = jnp.concatenate(
        [
            padded(scale * v, reactions, 0.0)
            for v in (
                yields[:, 0] + jnp.where(equal, yields[:, 1], 0.0),
                jnp.where(equal, 0.0, yields[:, 1]),
            )
        ]
    )
    more = reactions - real
    rrows = jnp.pad(
        jnp.concatenate([reactants, products], axis=1).T, ((0, 0), (0, more)), constant_values=-1
    )
    rcolumns = jnp.pad(reactants, ((0, more), (0, 0)), constant_values=-1)
    yrows = jnp.pad(yields.T, ((0, 0), (0, more)))
    rate_rows = jnp.pad(rates[:, 0, :], ((0, more), (0, 0)))
    conc = concentrations[:, 0, :]
    sens = tangents.reshape(group, species, cells // LANES, LANES)
    permute = jnp.asarray(table["permute"], BF16)

    short = -(-species // 8)
    rest = -(-species // 8) * 8
    per_group = [shape(NMAX, reactions, LANES)] * 3 + [shape(NMAX, species, LANES)] * 3
    work = [pltpu.VMEM((species + 1, group, LANES), F32)] * (2 + 2 * BUFFERS)
    raw = pltpu.VMEM((species, group // 8, cells // LANES, 8, LANES), F32)
    held = [pltpu.VMEM(s.shape, F32) for s in per_group]
    strip_rows, corner_rows = species * 8 + rest, short * 8 + rest

    outs = pl.pallas_call(
        edge_kernel,
        out_shape=[
            shape(species, group, LANES),
            shape(species, cells),
            shape(8, cells),
            *per_group,
            *([shape(strip_rows, LANES)] * 4),
            *([shape(corner_rows, LANES)] * 4),
        ],
        in_specs=[smem] * 3 + [vmem] * 9 + [hbm],
        out_specs=[vmem] * 17,
        scratch_shapes=[
            raw,
            *work[:2],
            *held,
            pltpu.VMEM((short * 8, 8, LANES), F32),
            pltpu.VMEM((6, species, reactions), BF16),
            pltpu.VMEM((2 * reactions, species), BF16),
            pltpu.VMEM((species, cells), F32),
            *work[2:],
            pltpu.SemaphoreType.DMA((group // 8,)),
        ],
        compiler_params=limit,
        name="edge_columns",
    )(
        ilist, ylist, reaction_index,
        conc, rate_rows, substeps, rrows, rcolumns, yrows, permute,
        jnp.asarray(table["strip"], BF16), jnp.asarray(table["corner"], BF16), sens,
    )
    t_a, conc_end, counts = outs[:3]
    held_b = outs[3:9]
    to_west, to_east, to_south, to_north = outs[9:13]
    tips = outs[13:17]

    h0 = passed_along(to_east, "tile", across)
    h1 = passed_along(to_west, "tile", -across)
    h2 = passed_along(to_north, "tile", 1)
    h3 = passed_along(to_south, "tile", -1)
    offsets = (across + 1, across - 1, -(across - 1), -(across + 1))
    corners = [passed_along(tip, "tile", by) for tip, by in zip(tips, offsets, strict=True)]

    t_b = pl.pallas_call(
        inner_kernel,
        out_shape=shape(species, group, LANES),
        in_specs=[smem] * 3 + [vmem] * 8 + [hbm],
        out_specs=vmem,
        scratch_shapes=[raw, *work, pltpu.SemaphoreType.DMA((group // 8,))],
        compiler_params=limit,
        name="inner_columns",
    )(ilist, ylist, reaction_index, counts, *held_b, permute, sens)

    result, conc_out = pl.pallas_call(
        advect_kernel,
        out_shape=[shape(group, species, cells // LANES, LANES), shape(species, cells)],
        in_specs=[vmem] * 18,
        out_specs=[hbm, vmem],
        scratch_shapes=[
            raw,
            pltpu.VMEM((short * 8, 8, LANES), F32),
            pltpu.VMEM((2, 4 * LANES, cells), BF16),
            pltpu.SemaphoreType.DMA,
        ],
        compiler_params=limit,
        name="advection",
    )(
        t_a, t_b, conc_end, h0, h1, h2, h3, *corners, cx, courant[1],
        jnp.asarray(table["columns"]), jnp.asarray(table["mid_rows"]),
        jnp.asarray(table["mid_columns"]), jnp.asarray(table["out_rows"]),
        jnp.asarray(table["conc_corner"], BF16),
    )
    return (
        conc_out.reshape(species, 1, cells),
        result.reshape(group, species, 1, cells),
    )


def solution(mesh):
    in_specs = (
        P(None, "tile", None),
        P("pgrp", None, "tile", None),
        P(None, "tile", None),
        P("tile", None),
        P(None, "tile", None),
        P(),
        P(),
        P(),
        P("pgrp"),
    )
    out_specs = (P(None, "tile", None), P("pgrp", None, "tile", None))
    return jax.shard_map(
        per_device, mesh=mesh, in_specs=in_specs, out_specs=out_specs, check_vma=False
    )
```

time: 468 us -> 155 us (0.33)
  the two profiles are of different devices: /device:TPU:13 before, /device:TPU:27 now
where the time goes in v1:
time: 155 us; the launch traced here: 154 us
  Pallas kernels  83.7 us (54%)
  waiting for transfers between devices  28.9 us (19%)
  starting transfers between devices  24.6 us (16%)
  local copies, waits for them, and re-layouts  13.1 us (8%)
  other arithmetic  2.69 us (2%)
    pallas_call x1, Pallas kernels, per_device(): pl.pallas_call(edge_kernel, out_shape=[shape(species, group, LANES), shap...  39 us
    pallas_call x1, Pallas kernels, per_device(): pl.pallas_call(inner_kernel, out_shape=shape(species, group, LANES), in_s...  30.9 us
    ppermute x10, waiting for transfers between devices, passed_along(): return lax.ppermute(value, axis, pairs)  28.9 us
    ppermute x10, starting transfers between devices, passed_along(): return lax.ppermute(value, axis, pairs)  24.6 us
    pallas_call x1, Pallas kernels, per_device(): pl.pallas_call(advect_kernel, out_shape=[shape(group, species, cells // L...  13.8 us
    unnamed x24, local copies, waits for them, and re-layouts  6.62 us
  transfers between devices with their start and end apart: 10, of which 5 were waited for; matrix products, arithmetic and copies ran while one was open for 1% of the time, Pallas kernels for 20%

profile of v1, /device:TPU:27, one launch (start us, length us, event | category | flops | bytes accessed | tf_op | source)
XLA Modules:
  0.0 153.8 jit_solution(7633029513458117810)
XLA Ops:
  0.6 0.0 copy-start.8
  0.6 0.8 fusion.3
  1.4 0.8 fusion.5
  2.2 0.8 fusion.4
  3.0 0.7 add_bitcast_fusion
  3.7 0.8 copy.24
  4.5 0.6 pad.43.rrows
  5.1 0.7 pad.44.rcolumns
  5.7 1.6 %copy.39 = f32[130,1,256]{2,0,1:T(8,128)} copy(f32[130,1,256]{2,1,0:T(1,128)} %param.17) | data formatting | bytes 266240
  7.3 1.0 copy.38
  8.3 1.3 pad.45.yrows
  9.5 0.7 pad.42.rates
  10.2 0.7 select_maximum_fusion.ylist
  10.9 0.7 select_add_fusion.ilist
  11.5 39.0 %edge_columns.1 = (f32[130,32,128]{2,1,0:T(8,128)}, f32[130,256]{1,0:T(8,128)}, f32[8,256]{1,0:T(8,128)}, f32[4,224,128]{2,1,0:T(8,128)}, f32[4,224,128]{2,1,0:T...) custom-call(s32[896]{0:T(1024)} %select_add_fusion.ilist, ...), custom_call_target="tpu_custom_call" | custom-call | tf_op jit(solution)/shard_map/edge_columns/pallas_call | solution.py:584
  50.6 1.3 collective-permute-start
  51.9 4.0 %collective-permute-start.1 = (f32[1176,128]{1,0:T(8,128)}, f32[1176,128]{1,0:T(8,128)S(1)}, u32[]{:S(2)}, u32[]{:S(2)}) collective-permute-start(f32[1176,128]{1,0:T(8,128)} %get-tuple-element.31), channel_id=1, source_target_pairs={{8,0},{10,2},{12,4},{14,6},{16,8},{18,10},{20,12},{22,14},{24,16},... | collective-permute-start | bytes 1806344 | tf_op jit(solution)/shard_map/ppermute | solution.py:515
  55.9 1.3 collective-permute-start.2
  57.2 3.1 %collective-permute-start.3 = (f32[1176,128]{1,0:T(8,128)}, f32[1176,128]{1,0:T(8,128)S(1)}, u32[]{:S(2)}, u32[]{:S(2)}) collective-permute-start(f32[1176,128]{1,0:T(8,128)} %get-tuple-element.33), channel_id=1, source_target_pairs={{2,0},{4,2},{6,4},{8,6},{10,8},{12,10},{14,12},{16,14},{18,16},{20... | collective-permute-start | bytes 1806344 | tf_op jit(solution)/shard_map/ppermute | solution.py:515
  60.3 0.0 copy-done.8
  60.3 0.6 slice_bitcast_fusion
  60.8 0.1 reshape_squeeze.3
  60.9 0.1 fusion.2
  61.0 0.1 copy.35
  61.1 0.1 reshape.21
  61.2 1.9 %collective-permute-start.9 = (f32[1,32]{1,0:T(1,128)S(1)}, f32[1,32]{1,0:T(1,128)S(1)}, u32[]{:S(2)}, u32[]{:S(2)}) collective-permute-start(f32[1,32]{1,0:T(1,128)S(1)} %reshape.21), channel_id=1, source_target_pairs={{2,0},{4,2},{6,4},{8,6},{10,8},{12,10},{14,12},{16,14},{18,16},{20... | collective-permute-start | bytes 392 | tf_op jit(solution)/shard_map/ppermute | solution.py:515
  63.1 0.1 copy.34
  63.1 0.1 reshape.20
  63.2 0.6 collective-permute-done.9
  63.9 1.3 collective-permute-start.8
  65.1 11.6 %collective-permute-done.8 = f32[1,32]{1,0:T(1,128)S(1)} collective-permute-done((f32[1,32]{1,0:T(1,128)S(1)}, f32[1,32]{1,0:T(1,128)S(1)}, u32[]{:S(2)}, u32[]{:S(2)}) %collective-permute-start.8) | collective-permute-done | bytes 160 | tf_op jit(solution)/shard_map/ppermute | solution.py:515
  76.7 1.3 collective-permute-start.4
  78.0 6.1 %collective-permute-done.4.d0 = f32[272,128]{1,0:T(8,128)S(1)} collective-permute-done((f32[272,128]{1,0:T(8,128)}, f32[272,128]{1,0:T(8,128)S(1)}, u32[]{:S(2)}, u32[]{:S(2)}) %collective-permute-start.4) | collective-permute-done | bytes 139296 | tf_op jit(solution)/shard_map/ppermute | solution.py:515
  84.1 0.0 copy-start.4
  84.1 1.3 collective-permute-start.5
  85.4 8.3 %collective-permute-done.5.d1 = f32[272,128]{1,0:T(8,128)S(1)} collective-permute-done((f32[272,128]{1,0:T(8,128)}, f32[272,128]{1,0:T(8,128)S(1)}, u32[]{:S(2)}, u32[]{:S(2)}) %collective-permute-start.5) | collective-permute-done | bytes 139296 | tf_op jit(solution)/shard_map/ppermute | solution.py:515
  93.7 0.0 copy-start.5
  93.7 3.3 %collective-permute-start.6 = (f32[272,128]{1,0:T(8,128)}, f32[272,128]{1,0:T(8,128)S(1)}, u32[]{:S(2)}, u32[]{:S(2)}) collective-permute-start(f32[272,128]{1,0:T(8,128)} %get-tuple-element.36), channel_id=1, source_target_pairs={{6,0},{8,2},{10,4},{12,6},{14,8},{16,10},{18,12},{20,14},{22,16},{... | collective-permute-start | bytes 417800 | tf_op jit(solution)/shard_map/ppermute | solution.py:515
  97.0 2.3 %collective-permute-done.6.d2 = f32[272,128]{1,0:T(8,128)S(1)} collective-permute-done((f32[272,128]{1,0:T(8,128)}, f32[272,128]{1,0:T(8,128)S(1)}, u32[]{:S(2)}, u32[]{:S(2)}) %collective-permute-start.6) | collective-permute-done | bytes 139296 | tf_op jit(solution)/shard_map/ppermute | solution.py:515
  99.3 0.0 copy-start.6
  99.3 5.9 %collective-permute-start.7 = (f32[272,128]{1,0:T(8,128)}, f32[272,128]{1,0:T(8,128)S(1)}, u32[]{:S(2)}, u32[]{:S(2)}) collective-permute-start(f32[272,128]{1,0:T(8,128)} %get-tuple-element.37), channel_id=1, source_target_pairs={{10,0},{12,2},{14,4},{16,6},{18,8},{20,10},{22,12},{24,14},{26,16}... | collective-permute-start | bytes 417800 | tf_op jit(solution)/shard_map/ppermute | solution.py:515
  105.2 0.1 pad.49.clone
  105.3 30.9 %inner_columns.1.t_b = f32[130,32,128]{2,1,0:T(8,128)} custom-call(s32[896]{0:T(1024)} %select_add_fusion.ilist, f32[448]{0:T(512)} %select_maximum_fusion.ylist, s32[32]{0:T(128)} %chosen.3, f32[8,256]{1,0:T(8,128)} %get-tuple-element.22.counts, f32[4,224,128]{2,1,0:T(8,128)} %get-tuple-element.23.a_b, f32[4,224,128]{2,1,0:T(8,128)} %get-tuple-element.24.b_b, ...), custom_call_target="tpu_custom_call" | custom-call | tf_op jit(solution)/shard_map/inner_columns/pallas_call | solution.py:626
  136.2 0.0 copy-done.4
  136.2 0.0 copy-done.5
  136.2 0.0 copy-done.6
  136.2 0.6 reshape_maximum_fusion.cx
  136.9 0.0 collective-permute-done.7.d3
  136.9 0.0 copy-start.7
  136.9 0.0 collective-permute-done.h0
  136.9 0.0 copy-start
  136.9 0.0 collective-permute-done.1.h1
  136.9 0.0 copy-start.1
  136.9 0.0 collective-permute-done.2.h2
  136.9 0.0 copy-start.2
  136.9 0.0 collective-permute-done.3.h3
  136.9 0.0 copy-start.3
  136.9 0.6 copy-done.7
  137.5 0.2 copy-done
  137.7 0.2 copy-done.1
  137.9 0.2 copy-done.2
  138.2 0.2 copy-done.3
  138.3 13.8 %advection.1 = (f32[32,130,2,128]{3,2,1,0:T(2,128)}, f32[130,256]{1,0:T(8,128)}) custom-call(f32[130,32,128]{2,1,0:T(8,128)} %get-tuple-element.21.t_a, f32[130,32,128]{2,1,0:T(8,128)} %inner_columns.1.t_b, f32[130,256]{1,0:T(8,128)} %get-tuple-element.29.conc, f32[1176,128]{1,0:T(8,128)} %copy-done, f32[1176,128]{1,0:T(8,128)} %copy-done.1, ...), custom_call_target="tpu_custom_call" | custom-call | tf_op jit(solution)/shard_map/advection/pallas_call | solution.py:636
  152.1 1.7 %copy.28 = f32[130,1,256]{2,1,0:T(1,128)} copy(f32[130,1,256]{2,0,1:T(8,128)} %bitcast.28) | data formatting | bytes 266240
  (4 shorter events, 0.0 us)
Async XLA Ops:
  0.6 59.6 %copy-start.8 = (f32[2,1,256]{2,1,0:T(1,128)S(1)}, f32[2,1,256]{2,1,0:T(1,128)}, u32[]{:S(2)}) copy-start(f32[2,1,256]{2,1,0:T(1,128)} %param.21) | copy-start | bytes 6148
  50.6 86.3 %collective-permute-start = (f32[1176,128]{1,0:T(8,128)}, f32[1176,128]{1,0:T(8,128)S(1)}, u32[]{:S(2)}, u32[]{:S(2)}) collective-permute-start(f32[1176,128]{1,0:T(8,128)} %get-tuple-element.30), channel_id=1, source_target_pairs={{0,8},{2,10},{4,12},{6,14},{8,16},{10,18},{12,20},{14,22},{16,24},... | collective-permute-start | bytes 1806344 | tf_op jit(solution)/shard_map/ppermute | solution.py:515
  51.9 85.0 %collective-permute-start.1 = (f32[1176,128]{1,0:T(8,128)}, f32[1176,128]{1,0:T(8,128)S(1)}, u32[]{:S(2)}, u32[]{:S(2)}) collective-permute-start(f32[1176,128]{1,0:T(8,128)} %get-tuple-element.31), channel_id=1, source_target_pairs={{8,0},{10,2},{12,4},{14,6},{16,8},{18,10},{20,12},{22,14},{24,16},... | collective-permute-start | bytes 1806344 | tf_op jit(solution)/shard_map/ppermute | solution.py:515
  55.9 81.0 %collective-permute-start.2 = (f32[1176,128]{1,0:T(8,128)}, f32[1176,128]{1,0:T(8,128)S(1)}, u32[]{:S(2)}, u32[]{:S(2)}) collective-permute-start(f32[1176,128]{1,0:T(8,128)} %get-tuple-element.32), channel_id=1, source_target_pairs={{0,2},{2,4},{4,6},{6,8},{8,10},{10,12},{12,14},{14,16},{16,18},{18... | collective-permute-start | bytes 1806344 | tf_op jit(solution)/shard_map/ppermute | solution.py:515
  57.2 79.7 %collective-permute-start.3 = (f32[1176,128]{1,0:T(8,128)}, f32[1176,128]{1,0:T(8,128)S(1)}, u32[]{:S(2)}, u32[]{:S(2)}) collective-permute-start(f32[1176,128]{1,0:T(8,128)} %get-tuple-element.33), channel_id=1, source_target_pairs={{2,0},{4,2},{6,4},{8,6},{10,8},{12,10},{14,12},{16,14},{18,16},{20... | collective-permute-start | bytes 1806344 | tf_op jit(solution)/shard_map/ppermute | solution.py:515
  61.2 2.7 %collective-permute-start.9 = (f32[1,32]{1,0:T(1,128)S(1)}, f32[1,32]{1,0:T(1,128)S(1)}, u32[]{:S(2)}, u32[]{:S(2)}) collective-permute-start(f32[1,32]{1,0:T(1,128)S(1)} %reshape.21), channel_id=1, source_target_pairs={{2,0},{4,2},{6,4},{8,6},{10,8},{12,10},{14,12},{16,14},{18,16},{20... | collective-permute-start | bytes 392 | tf_op jit(solution)/shard_map/ppermute | solution.py:515
  63.9 12.9 %collective-permute-start.8 = (f32[1,32]{1,0:T(1,128)S(1)}, f32[1,32]{1,0:T(1,128)S(1)}, u32[]{:S(2)}, u32[]{:S(2)}) collective-permute-start(f32[1,32]{1,0:T(1,128)S(1)} %reshape.20), channel_id=1, source_target_pairs={{0,2},{2,4},{4,6},{6,8},{8,10},{10,12},{12,14},{14,16},{16,18},{18... | collective-permute-start | bytes 392 | tf_op jit(solution)/shard_map/ppermute | solution.py:515
  76.7 7.4 %collective-permute-start.4 = (f32[272,128]{1,0:T(8,128)}, f32[272,128]{1,0:T(8,128)S(1)}, u32[]{:S(2)}, u32[]{:S(2)}) collective-permute-start(f32[272,128]{1,0:T(8,128)} %get-tuple-element.34), channel_id=1, source_target_pairs={{0,10},{2,12},{4,14},{6,16},{8,18},{10,20},{12,22},{14,24},{16,26}... | collective-permute-start | bytes 417800 | tf_op jit(solution)/shard_map/ppermute | solution.py:515
  84.1 52.1 %copy-start.4 = (f32[272,128]{1,0:T(8,128)}, f32[272,128]{1,0:T(8,128)S(1)}, u32[]{:S(2)}) copy-start(f32[272,128]{1,0:T(8,128)S(1)} %collective-permute-done.4.d0) | copy-start | bytes 417796
  84.1 9.6 %collective-permute-start.5 = (f32[272,128]{1,0:T(8,128)}, f32[272,128]{1,0:T(8,128)S(1)}, u32[]{:S(2)}, u32[]{:S(2)}) collective-permute-start(f32[272,128]{1,0:T(8,128)} %get-tuple-element.35), channel_id=1, source_target_pairs={{0,6},{2,8},{4,10},{6,12},{8,14},{10,16},{12,18},{14,20},{16,22},{... | collective-permute-start | bytes 417800 | tf_op jit(solution)/shard_map/ppermute | solution.py:515
  93.7 42.5 %copy-start.5 = (f32[272,128]{1,0:T(8,128)}, f32[272,128]{1,0:T(8,128)S(1)}, u32[]{:S(2)}) copy-start(f32[272,128]{1,0:T(8,128)S(1)} %collective-permute-done.5.d1) | copy-start | bytes 417796
  93.7 5.7 %collective-permute-start.6 = (f32[272,128]{1,0:T(8,128)}, f32[272,128]{1,0:T(8,128)S(1)}, u32[]{:S(2)}, u32[]{:S(2)}) collective-permute-start(f32[272,128]{1,0:T(8,128)} %get-tuple-element.36), channel_id=1, source_target_pairs={{6,0},{8,2},{10,4},{12,6},{14,8},{16,10},{18,12},{20,14},{22,16},{... | collective-permute-start | bytes 417800 | tf_op jit(solution)/shard_map/ppermute | solution.py:515
  99.3 36.9 %copy-start.6 = (f32[272,128]{1,0:T(8,128)}, f32[272,128]{1,0:T(8,128)S(1)}, u32[]{:S(2)}) copy-start(f32[272,128]{1,0:T(8,128)S(1)} %collective-permute-done.6.d2) | copy-start | bytes 417796
  99.3 37.5 %collective-permute-start.7 = (f32[272,128]{1,0:T(8,128)}, f32[272,128]{1,0:T(8,128)S(1)}, u32[]{:S(2)}, u32[]{:S(2)}) collective-permute-start(f32[272,128]{1,0:T(8,128)} %get-tuple-element.37), channel_id=1, source_target_pairs={{10,0},{12,2},{14,4},{16,6},{18,8},{20,10},{22,12},{24,14},{26,16}... | collective-permute-start | bytes 417800 | tf_op jit(solution)/shard_map/ppermute | solution.py:515
  136.9 0.7 copy-start.7
  136.9 0.9 copy-start
  136.9 1.0 copy-start.1
  136.9 1.3 copy-start.2
  136.9 1.4 copy-start.3

commit v2 on v1

v2 whole, which is shorter than its diff:
```python
import functools
import math

import jax
import jax.numpy as jnp
import numpy as np
from jax import lax
from jax.experimental import pallas as pl
from jax.experimental.pallas import tpu as pltpu
from jax.sharding import PartitionSpec as P

CX = 16
CY = 16
NMAX = 4
LANES = 128
UNROLL = 8
BUFFERS = 2
SPLIT = 2
F32 = jnp.float32
BF16 = jnp.bfloat16


def orders():
    last, end = CX - 2, CY - 2
    west = [(i, j) for i in range(2) for j in range(CY)]
    east = [(i, j) for i in range(last, CX) for j in range(CY)]
    south = [(i, j) for j in range(2) for i in range(CX)]
    north = [(i, j) for j in range(end, CY) for i in range(CX)]
    strips = west + east + south + north
    edge = list(dict.fromkeys(strips))
    inner = [(i, j) for i in range(CX) for j in range(CY) if (i, j) not in set(edge)]
    return edge + inner, strips


def one_hot(source, wanted):
    place = {cell: k for k, cell in enumerate(source)}
    table = np.zeros((len(source), len(wanted)), np.float32)
    for lane, cell in enumerate(wanted):
        if cell is not None:
            table[place[cell], lane] = 1.0
    return table


def static_tables():
    order, strips = orders()
    cells = [(i, j) for i in range(CX) for j in range(CY)]
    west = [(i - CX, j) for i, j in strips[32:64]]
    east = [(i + CX, j) for i, j in strips[0:32]]
    south = [(i, j - CY) for i, j in strips[96:128]]
    north = [(i, j + CY) for i, j in strips[64:96]]
    blocks = [order[32 * k : 32 * k + 32] for k in range(4)] + [west, east]
    side_in = [(i, j, q) for block in blocks for q in range(4) for i, j in block]
    own_sides = (strips[64:96], strips[96:128])
    side_out = [(i, j, q) for block in own_sides for q in range(4) for i, j in block]
    entries = order + west + east + south + north
    return {
        "permute": one_hot(cells, order),
        "side_pick": one_hot(cells, [(i, j) for i, j, _ in side_out]),
        "side_in": np.array(side_in, np.int32),
        "side_out": np.array(side_out, np.int32).T,
        "entries": np.array(entries, np.int32),
        "cells": np.array(cells, np.int32),
        "cells_rows": np.array(cells, np.int32).T,
    }


def dot(left, right):
    return jnp.dot(left, right, preferred_element_type=F32)


def parts_of(value, count):
    parts = []
    for k in range(count):
        part = value.astype(BF16)
        parts.append(part)
        if k + 1 < count:
            value = value - part.astype(F32)
    return parts


def select_left(exact, value, count):
    return sum(dot(exact, part) for part in parts_of(value, count))


def select_right(value, exact, count):
    return sum(dot(part, exact) for part in parts_of(value, count))


def product(left_parts, value):
    high, low = parts_of(value, 2)
    return dot(left_parts[0], high) + (dot(left_parts[0], low) + dot(left_parts[1], high))


def product_right(value, right_parts):
    high, low = parts_of(value, 2)
    return dot(high, right_parts[0]) + (dot(low, right_parts[0]) + dot(high, right_parts[1]))


def lane_of(rows):
    return lax.broadcasted_iota(jnp.int32, (rows, LANES), 1)


def swap_blocks(arrays):
    lane = lane_of(arrays[0].shape[0])
    low = lane < 64
    even = (lane // 32) % 2 == 0
    a, b, c, d = arrays
    a, c = (
        jnp.where(low, a, pltpu.roll(c, 64, 1)),
        jnp.where(low, pltpu.roll(a, 64, 1), c),
    )
    b, d = (
        jnp.where(low, b, pltpu.roll(d, 64, 1)),
        jnp.where(low, pltpu.roll(b, 64, 1), d),
    )
    a, b = (
        jnp.where(even, a, pltpu.roll(b, 32, 1)),
        jnp.where(even, pltpu.roll(a, 96, 1), b),
    )
    c, d = (
        jnp.where(even, c, pltpu.roll(d, 32, 1)),
        jnp.where(even, pltpu.roll(c, 96, 1), d),
    )
    return [a, b, c, d]


def tangent_copies(source, target, sems):
    return [
        pltpu.make_async_copy(source.at[p], target.at[:, p // 8, :, p % 8, :], sems.at[p // 8])
        for p in range(source.shape[0])
    ]


def up_to(value, step):
    return -(-value // step) * step


def rows_of(reactions, species):
    padded = up_to(species, 8)
    starts = [0, reactions, 2 * reactions]
    starts += [3 * reactions + k * padded for k in range(3)]
    return starts, 3 * reactions + 3 * padded


def several(count):
    return max(k for k in range(1, 14) if count % k == 0)


def tangent_chemistry(ilist, ylist, chosen, held, reactions, t, x, used, made, start, stop, base):
    species = t.shape[0] - 1
    group = t.shape[1]
    (at_a, at_b, at_flux, at_fd, at_fda, at_again), _ = rows_of(reactions, species)
    sublane = lax.broadcasted_iota(jnp.int32, (8, LANES), 0)
    batch = several(species)

    def apply(source, n):
        def body(step, carry):
            mixes, places = [], []
            for k in range(UNROLL):
                r = step * UNROLL + k
                place = [ilist[row, r] for row in range(4)]
                mixes.append(
                    held[n, pl.ds(at_a + r, 1), :] * source[place[0]]
                    + held[n, pl.ds(at_b + r, 1), :] * source[place[1]]
                )
                places.append(place)
            for k0 in range(0, UNROLL, BUFFERS):
                olds = []
                for k in range(BUFFERS):
                    i1, i2, q1, q2 = places[k0 + k]
                    olds.append((used[k][i1], used[k][i2], made[k][q1], made[k][q2]))
                for k in range(BUFFERS):
                    r = step * UNROLL + k0 + k
                    i1, i2, q1, q2 = places[k0 + k]
                    mix, old = mixes[k0 + k], olds[k]
                    used[k][i1] = old[0] - mix
                    used[k][i2] = old[1] - mix
                    made[k][q1] = old[2] + ylist[0, r] * mix
                    made[k][q2] = old[3] + ylist[1, r] * mix
            return carry

        lax.fori_loop(0, reactions // UNROLL, body, 0)

    def force(n):
        def body(p8, carry):
            at = sublane == p8
            for q in range(group // 8):
                r = chosen[q * 8 + p8]
                value = jnp.where(at, held[n, pl.ds(at_flux + r, 1), :], 0.0)
                i1, i2, q1, q2 = [ilist[row, r] for row in range(4)]
                lost, gained = used[q % BUFFERS], made[q % BUFFERS]
                rows = slice(q * 8, (q + 1) * 8)
                one, two = lost[i1, rows, :], lost[i2, rows, :]
                three, four = gained[q1, rows, :], gained[q2, rows, :]
                lost[i1, rows, :] = one - value
                lost[i2, rows, :] = two - value
                gained[q1, rows, :] = three + ylist[0, r] * value
                gained[q2, rows, :] = four + ylist[1, r] * value
            return carry

        lax.fori_loop(0, 8, body, 0)

    def total(s):
        value = used[0][s] + made[0][s]
        for k in range(1, BUFFERS):
            value = value + (used[k][s] + made[k][s])
        return value

    def each(work, target):
        def body(step, carry):
            news = [work(step * batch + k) for k in range(batch)]
            for k, (value, kept) in enumerate(news):
                target[step * batch + k] = value
                used[0][step * batch + k] = kept
            return carry

        lax.fori_loop(0, species // batch, body, 0)

    def substep(index, carry):
        n = index - base
        force(n)
        apply(t, n)

        def first(s):
            right = total(s)
            value = right * held[n, pl.ds(at_fd + s, 1), :]
            return value, used[0][s] + right * held[n, pl.ds(at_again + s, 1), :]

        each(first, x)
        apply(x, n)

        def second(s):
            right = total(s)
            return t[s] + right * held[n, pl.ds(at_fda + s, 1), :], used[0][s] - right

        each(second, t)
        return carry

    lax.fori_loop(start, stop, substep, 0)


def clear(refs):
    zero = jnp.zeros(refs[0].shape[1:], F32)

    def body(s, carry):
        for ref in refs:
            ref[s] = zero
        return carry

    lax.fori_loop(0, refs[0].shape[0], body, 0)


def weights(c):
    g = c * (1.0 - c * c) / 6.0
    up = c > 0
    half, square = 0.5 * c, 0.5 * c * c
    return (
        jnp.where(up, -g, 0.0),
        half + square + jnp.where(up, 3.0 * g, -g),
        1.0 - c * c + jnp.where(up, -3.0 * g, 3.0 * g),
        square - half + jnp.where(up, g, -3.0 * g),
        jnp.where(up, 0.0, g),
    )


def edge_kernel(
    chosen, reactants, products, yields, counts, permute, conc, rates, tangents,
    ilist_out, ylist_out, counts_out, conc_out, t_out, t_b, held_b, s0, s1, s2, s3,
    raw, t, x, held, other, inner, conc_in, rates_in, pairs, net_parts, hot, base,
    ilist, ylist, *rest,
):
    sems = rest[-1]
    used, made = list(rest[:BUFFERS]), list(rest[BUFFERS : 2 * BUFFERS])
    species, real = conc.shape[0], rates.shape[0]
    reactions = rates_in.shape[1]
    halves = conc_in.shape[0]
    starts, _ = rows_of(reactions, species)
    aligned = real // 8 * 8
    for half in range(halves):
        rates_in[half, aligned:] = jnp.zeros((reactions - aligned, LANES), F32)
    small = [
        pltpu.make_async_copy(conc.at[:, half, :], conc_in.at[half], sems.at[4])
        for half in range(halves)
    ] + [
        pltpu.make_async_copy(rates.at[:, half, :], rates_in.at[half, 0:real, :], sems.at[5])
        for half in range(halves)
    ]
    copies = tangent_copies(tangents, raw, sems)
    for copy in small + copies:
        copy.start()

    pairs[...] = jnp.full(pairs.shape, -1, jnp.int32)
    pairs[0:2, 0:real] = reactants[...]
    pairs[2:4, 0:real] = products[...]
    ylist_out[...] = jnp.zeros(ylist_out.shape, F32)
    ylist_out[0:2, 0:real] = yields[...]
    r0, r1, p0, p1 = [pairs[k : k + 1, :] for k in range(4)]
    y0, y1 = ylist_out[0:1, :], ylist_out[1:2, :]
    same, equal = r0 == r1, p0 == p1
    scale = jnp.where(same, 0.5, 1.0)
    for k, value in enumerate(
        (r0, jnp.where(same, species, r1), p0, jnp.where(equal, species, p1))
    ):
        ilist_out[k : k + 1, :] = jnp.where(r0 < 0, species, value)
    ilist_out[4:8, :] = jnp.zeros((4, pairs.shape[1]), jnp.int32)
    ylist_out[0:1, :] = scale * (y0 + jnp.where(equal, y1, 0.0))
    ylist_out[1:2, :] = scale * jnp.where(equal, 0.0, y1)
    lists = [
        pltpu.make_async_copy(ilist_out, ilist, sems.at[6]),
        pltpu.make_async_copy(ylist_out, ylist, sems.at[7]),
    ]
    for copy in lists:
        copy.start()

    row = lax.broadcasted_iota(jnp.int32, (species, reactions), 0)
    r0, r1, p0, p1 = [value[:, 0:reactions] for value in (r0, r1, p0, p1)]
    y0, y1 = y0[:, 0:reactions], y1[:, 0:reactions]
    uses_one = row == r0
    uses_two = row == r1
    net = (
        jnp.where(row == p0, y0, 0.0)
        + jnp.where(row == p1, y1, 0.0)
        - jnp.where(uses_one, 1.0, 0.0)
        - jnp.where(uses_two, 1.0, 0.0)
    )
    for k, value in enumerate((net, jnp.where(uses_one, net, 0.0), jnp.where(uses_two, net, 0.0))):
        high, low = parts_of(value, 2)
        net_parts[2 * k] = high
        net_parts[2 * k + 1] = low
    lane = lane_of(reactions)
    columns = []
    for k in range(2):
        column = jnp.transpose(jnp.broadcast_to(pairs[k : k + 1, :], (LANES, pairs.shape[1])))
        column = column[0:reactions]
        columns.append(column[:, 0:1])
        for at in range(0, species, LANES):
            width = min(LANES, species - at)
            value = jnp.where(column == lane + at, 1.0, 0.0)[:, 0:width]
            hot[k * reactions : (k + 1) * reactions, at : at + width] = value.astype(BF16)
    same = columns[0] == columns[1]

    order = permute[...]
    count = dot(jnp.broadcast_to(counts[...].astype(F32), (8, counts.shape[1])).astype(BF16), order)
    counts_out[...] = count
    count = count[0:1, :]
    factor = 1.0 / count
    highest = jnp.max(count).astype(jnp.int32)
    for copy in small:
        copy.wait()
    base[...] = select_right(jnp.concatenate([conc_in[0], conc_in[1]], axis=1), order, 3)
    rate = select_right(jnp.concatenate([rates_in[0], rates_in[1]], axis=1), order, 3)

    def keep(n, k, value):
        rows = slice(starts[k], starts[k] + value.shape[0])
        held[n, rows, :] = value[:, :LANES]
        other[n, rows, :] = value[:, LANES:]

    def substep(n, carry):
        c = base[...]
        picked = select_left(hot[...], c, 3)
        one, two = picked[:reactions], picked[reactions:]
        a = rate * two
        b = rate * one
        flux = a * one
        nets = (net_parts[0], net_parts[1])
        diagonal = product((net_parts[2], net_parts[3]), a) + product(
            (net_parts[4], net_parts[5]), b
        )
        change = product(nets, flux)
        divisor = 1.0 - factor * diagonal
        fd = factor / divisor
        start = fd * change
        along = select_left(hot[...], start, 2)
        again = product(nets, a * along[:reactions] + b * along[reactions:])
        move = fd * (change + (again - diagonal * start))
        active = n.astype(F32) < count
        base[...] = c + jnp.where(active, move, 0.0)
        keep(n, 0, jnp.where(same, 2.0 * (a + b), a))
        keep(n, 1, jnp.where(same, 0.0, b))
        keep(n, 2, jnp.where(same, 2.0 * flux, flux))
        keep(n, 3, fd)
        keep(n, 4, jnp.where(active, fd, 0.0))
        keep(n, 5, fd * (count - 2.0 * diagonal) - 1.0)
        return carry

    lax.fori_loop(0, highest, substep, 0)
    conc_out[...] = base[...]
    tables = pltpu.make_async_copy(other, held_b, sems.at[8])
    tables.start()

    for copy in copies:
        copy.wait()
    for q in range(raw.shape[1]):
        both = jnp.concatenate(
            [raw[:, q, half].reshape(species * 8, LANES) for half in range(halves)], axis=1
        )
        picked = select_right(both, order, 2)
        rows = slice(q * 8, (q + 1) * 8)
        t[0:species, rows, :] = picked[:, :LANES].reshape(species, 8, LANES)
        inner[:, rows, :] = picked[:, LANES:].reshape(species, 8, LANES)
    inner_out = pltpu.make_async_copy(inner, t_b, sems.at[9])
    inner_out.start()
    t[species] = jnp.zeros(t.shape[1:], F32)
    clear([x, *used, *made])
    for copy in lists:
        copy.wait()
    own = jnp.max(count[:, :LANES]).astype(jnp.int32)
    tangent_chemistry(ilist, ylist, chosen, held, reactions, t, x, used, made, 0, own, 0)
    t_out[...] = t[0:species]

    rows = species * 8
    tail = s0.shape[0] - rows
    strips = swap_blocks(
        [t[0:species, q * 8 : (q + 1) * 8, :].reshape(rows, LANES) for q in range(4)]
    )
    zero = jnp.zeros((species, LANES), F32)
    tails = swap_blocks([base[:, 0:LANES], zero, zero, zero])
    for ref, value, last in zip((s0, s1, s2, s3), strips, tails, strict=True):
        ref[0:rows] = value
        ref[rows:] = jnp.zeros((tail, LANES), F32)
        ref[rows : rows + species] = last
    tables.wait()
    inner_out.wait()


def section(di, dj, c):
    value = jnp.zeros(di.shape, F32)
    for k, weight in enumerate(weights(c)):
        value = jnp.where((di == k - 2) & (dj == 0), weight, value)
    return value


def inner_kernel(
    ilist, ylist, chosen, counts, courant, side_pick, side_in, side_out, s0, s1, s2, s3,
    held_b, t_b,
    t_out, part, side_high, side_low,
    held, t, x, *rest,
):
    sems = rest[-1]
    used, made = list(rest[:BUFFERS]), list(rest[BUFFERS : 2 * BUFFERS])
    species = t_b.shape[0]
    copies = [
        pltpu.make_async_copy(t_b, t.at[0:species], sems.at[0]),
        pltpu.make_async_copy(held_b.at[0:SPLIT], held, sems.at[1]),
    ]
    for copy in copies:
        copy.start()

    cx = jnp.concatenate([courant[0:1, :], courant[1:2, :]], axis=1)
    c = select_right(jnp.broadcast_to(cx, (8, cx.shape[1])), side_pick[...], 3)[0:1, :]
    di = side_in[:, 0:1] - side_out[0:1, :]
    dj = side_in[:, 1:2] - side_out[1:2, :]
    map_ = jnp.where(side_in[:, 2:3] == side_out[2:3, :], section(di, dj, c), 0.0)
    high, low = parts_of(map_, 2)
    near = 4 * LANES
    side_high[...] = high[near:]
    side_low[...] = low[near:]
    strips = jnp.concatenate([s0[...], s1[...], s2[...], s3[...]], axis=1)
    part[...] = product_right(strips, (high[:near], low[:near]))

    t[species] = jnp.zeros(t.shape[1:], F32)
    clear([x, *used, *made])
    for copy in copies:
        copy.wait()
    own = jnp.max(counts[0:1, LANES:]).astype(jnp.int32)
    tangent_chemistry(
        ilist, ylist, chosen, held, reactions_of(held, species), t, x, used, made,
        0, jnp.minimum(own, SPLIT), 0,
    )
    copy = pltpu.make_async_copy(t.at[0:species], t_out, sems.at[0])
    copy.start()
    copy.wait()


def reactions_of(held, species):
    return (held.shape[1] - 3 * up_to(species, 8)) // 3


def side_kernel(part, west, east, side_high, side_low, to_south, to_north):
    both = jnp.concatenate([west[...], east[...]], axis=1)
    value = part[...] + product_right(both, (side_high[...], side_low[...]))
    to_south[...] = value[:, :LANES]
    to_north[...] = value[:, LANES:]


def later_kernel(ilist, ylist, chosen, counts, held_b, t_b, t_out, held, t, x, *rest):
    sems = rest[-1]
    used, made = list(rest[:BUFFERS]), list(rest[BUFFERS : 2 * BUFFERS])
    species = t_b.shape[0]
    copies = [
        pltpu.make_async_copy(t_b, t.at[0:species], sems.at[0]),
        pltpu.make_async_copy(held_b.at[SPLIT:], held, sems.at[1]),
    ]
    for copy in copies:
        copy.start()
    t[species] = jnp.zeros(t.shape[1:], F32)
    clear([x, *used, *made])
    for copy in copies:
        copy.wait()
    own = jnp.max(counts[0:1, LANES:]).astype(jnp.int32)
    tangent_chemistry(
        ilist, ylist, chosen, held, reactions_of(held, species), t, x, used, made,
        SPLIT, own, SPLIT,
    )
    copy = pltpu.make_async_copy(t.at[0:species], t_out, sems.at[0])
    copy.start()
    copy.wait()


def advect_kernel(
    conc, h0, h1, h2, h3, courant, entries, cells, cells_rows, t_a, t_b,
    t_out, conc_out,
    first_in, second_in, done, conc_done, sems,
):
    species = conc.shape[0]
    rows = species * 8
    loads = []
    for q in range(4):
        part = slice(q * 8, (q + 1) * 8)
        loads.append(
            [
                pltpu.make_async_copy(t_a.at[:, part, :], first_in.at[q], sems.at[q]),
                pltpu.make_async_copy(t_b.at[:, part, :], second_in.at[q], sems.at[q]),
            ]
        )
        for copy in loads[q]:
            copy.start()

    cx = jnp.concatenate([courant[0:1, :], courant[1:2, :]], axis=1)
    cy = jnp.concatenate([courant[2:3, :], courant[3:4, :]], axis=1)
    di = entries[:, 0:1] - cells_rows[0:1, :]
    dj = entries[:, 1:2] - cells_rows[1:2, :]
    along_x = section(di, dj, cx)
    late = lax.broadcasted_iota(jnp.int32, di.shape, 0) >= di.shape[0] - 64
    along_y = jnp.where(late, section(dj, di, cy), 0.0)
    both = section(cells[:, 1:2] - cells_rows[1:2, :], cells[:, 0:1] - cells_rows[0:1, :], cy)
    whole = along_y + jnp.dot(
        along_x, both, precision=lax.Precision.HIGHEST, preferred_element_type=F32
    )
    high, low = parts_of(whole, 2)
    own = 2 * LANES
    local, outer = (high[:own], low[:own]), (high[own:], low[own:])

    halo = swap_blocks([h0[...], h1[...], h2[...], h3[...]])
    base = product_right(conc[...], local) + product_right(halo[0][rows : rows + species], outer)
    copies = []
    for half in range(2):
        conc_done[half] = base[:, half * LANES : (half + 1) * LANES]
        copies.append(
            pltpu.make_async_copy(conc_done.at[half], conc_out.at[:, half, :], sems.at[5])
        )
        copies[-1].start()
    for q in range(4):
        for copy in loads[q]:
            copy.wait()
        inside = jnp.concatenate(
            [first_in[q].reshape(rows, LANES), second_in[q].reshape(rows, LANES)], axis=1
        )
        value = product_right(inside, local) + product_right(halo[q][0:rows], outer)
        for half in range(2):
            done[:, q, half] = value[:, half * LANES : (half + 1) * LANES].reshape(
                species, 8, LANES
            )
        for p8 in range(8):
            copies.append(
                pltpu.make_async_copy(done.at[:, q, :, p8, :], t_out.at[q * 8 + p8], sems.at[4])
            )
            copies[-1].start()
    for copy in copies:
        copy.wait()


def passed_along(value, axis, by):
    size = lax.axis_size(axis)
    pairs = [(i, i + by) for i in range(size) if 0 <= i + by < size]
    return lax.ppermute(value, axis, pairs)


def per_device(
    concentrations, tangents, rates, substeps, courant, reactants, products, yields, reaction_index
):
    species = concentrations.shape[0]
    cells = CX * CY
    halves = cells // LANES
    group = tangents.shape[0]
    real = rates.shape[0]
    reactions = up_to(real, UNROLL)
    listed = up_to(reactions, LANES)
    across = math.isqrt(lax.axis_size("tile"))
    table = static_tables()
    vmem = pl.BlockSpec(memory_space=pltpu.VMEM)
    smem = pl.BlockSpec(memory_space=pltpu.SMEM)
    hbm = pl.BlockSpec(memory_space=pl.ANY)
    limit = pltpu.CompilerParams(vmem_limit_bytes=48 * 2**20)
    _, held_rows = rows_of(reactions, species)

    def shape(*sizes, dtype=F32):
        return jax.ShapeDtypeStruct(sizes, dtype)

    def bits(name):
        return jnp.asarray(table[name], BF16)

    conc = concentrations.reshape(species, halves, LANES)
    sens = tangents.reshape(group, species, halves, LANES)
    rate_rows = rates.reshape(real, halves, LANES)
    numbers = courant.reshape(2 * halves, LANES)

    state = shape(species, group, LANES)
    strip = shape(species * 8 + up_to(species, 8), LANES)
    wide = shape(strip.shape[0], 2 * LANES)
    held = shape(NMAX, held_rows, LANES)
    work = [pltpu.VMEM((species + 1, group, LANES), F32)] * (2 + 2 * BUFFERS)
    raw = pltpu.VMEM((species, group // 8, halves, 8, LANES), F32)

    ilist, ylist, counts, conc_end, t_a, t_b, held_b, s0, s1, s2, s3 = pl.pallas_call(
        edge_kernel,
        out_shape=[
            shape(8, listed, dtype=jnp.int32),
            shape(8, listed),
            shape(8, cells),
            shape(species, cells),
            state,
            state,
            held,
            *([strip] * 4),
        ],
        in_specs=[smem] + [vmem] * 5 + [hbm] * 3,
        out_specs=[vmem] * 5 + [hbm] * 2 + [vmem] * 4,
        scratch_shapes=[
            raw,
            *work[:2],
            pltpu.VMEM(held.shape, F32),
            pltpu.VMEM(held.shape, F32),
            pltpu.VMEM(state.shape, F32),
            pltpu.VMEM((halves, species, LANES), F32),
            pltpu.VMEM((halves, reactions, LANES), F32),
            pltpu.VMEM((8, listed), jnp.int32),
            pltpu.VMEM((6, species, reactions), BF16),
            pltpu.VMEM((2 * reactions, species), BF16),
            pltpu.VMEM((species, cells), F32),
            pltpu.SMEM((8, listed), jnp.int32),
            pltpu.SMEM((8, listed), F32),
            *work[2:],
            pltpu.SemaphoreType.DMA((10,)),
        ],
        compiler_params=limit,
        name="edge_columns",
    )(
        reaction_index, reactants.T, products.T, yields.T, substeps, bits("permute"),
        conc, rate_rows, sens,
    )

    west = passed_along(s1, "tile", across)
    east = passed_along(s0, "tile", -across)

    inner_scratch = [
        pltpu.VMEM((SPLIT, held_rows, LANES), F32),
        *work,
        pltpu.SemaphoreType.DMA((2,)),
    ]
    t_b, part, side_high, side_low = pl.pallas_call(
        inner_kernel,
        out_shape=[state, wide] + [shape(2 * LANES, 2 * LANES, dtype=BF16)] * 2,
        in_specs=[smem] * 3 + [vmem] * 9 + [hbm] * 2,
        out_specs=[hbm] + [vmem] * 3,
        scratch_shapes=inner_scratch,
        compiler_params=limit,
        name="inner_columns",
    )(
        ilist, ylist, reaction_index, counts, numbers, bits("side_pick"),
        jnp.asarray(table["side_in"]), jnp.asarray(table["side_out"]), s0, s1, s2, s3,
        held_b, t_b,
    )

    to_south, to_north = pl.pallas_call(
        side_kernel,
        out_shape=[strip, strip],
        in_specs=[vmem] * 5,
        out_specs=[vmem] * 2,
        compiler_params=limit,
        name="y_edges",
    )(part, west, east, side_high, side_low)
    south = passed_along(to_north, "tile", 1)
    north = passed_along(to_south, "tile", -1)

    t_b = pl.pallas_call(
        later_kernel,
        out_shape=state,
        in_specs=[smem] * 3 + [vmem] + [hbm] * 2,
        out_specs=hbm,
        scratch_shapes=inner_scratch,
        compiler_params=limit,
        name="inner_later",
    )(ilist, ylist, reaction_index, counts, held_b, t_b)

    result, conc_out = pl.pallas_call(
        advect_kernel,
        out_shape=[shape(group, species, halves, LANES), shape(species, halves, LANES)],
        in_specs=[vmem] * 9 + [hbm] * 2,
        out_specs=[hbm, hbm],
        scratch_shapes=[
            pltpu.VMEM((group // 8, species, 8, LANES), F32),
            pltpu.VMEM((group // 8, species, 8, LANES), F32),
            raw,
            pltpu.VMEM((halves, species, LANES), F32),
            pltpu.SemaphoreType.DMA((6,)),
        ],
        compiler_params=limit,
        name="advection",
    )(
        conc_end, west, east, south, north, numbers,
        jnp.asarray(table["entries"]), jnp.asarray(table["cells"]),
        jnp.asarray(table["cells_rows"]), t_a, t_b,
    )
    return (
        conc_out.reshape(species, 1, cells),
        result.reshape(group, species, 1, cells),
    )


def solution(mesh):
    in_specs = (
        P(None, "tile", None),
        P("pgrp", None, "tile", None),
        P(None, "tile", None),
        P("tile", None),
        P(None, "tile", None),
        P(),
        P(),
        P(),
        P("pgrp"),
    )
    out_specs = (P(None, "tile", None), P("pgrp", None, "tile", None))
    return jax.shard_map(
        per_device, mesh=mesh, in_specs=in_specs, out_specs=out_specs, check_vma=False
    )
```

time: 155 us -> 103 us (0.66)
  the two profiles are of different devices: /device:TPU:27 before, /device:TPU:30 now
where the time goes in v2:
time: 103 us; the launch traced here: 102 us
  Pallas kernels  82 us (80%)
  starting transfers between devices  11.4 us (11%)
  local copies, waits for them, and re-layouts  7.48 us (7%)
    pallas_call x1, Pallas kernels, per_device(): pl.pallas_call(edge_kernel, out_shape=[shape(8, listed, dtype=jnp.int32),...  37.7 us
    pallas_call x1, Pallas kernels, per_device(): pl.pallas_call(inner_kernel, out_shape=[state, wide] + [shape(2 * LANES,...  18 us
    pallas_call x1, Pallas kernels, per_device(): pl.pallas_call(later_kernel, out_shape=state, in_specs=[smem] * 3 + [vmem...  15.4 us
    ppermute x4, starting transfers between devices, passed_along(): return lax.ppermute(value, axis, pairs)  11.4 us
    pallas_call x1, Pallas kernels, per_device(): pl.pallas_call(advect_kernel, out_shape=[shape(group, species, halves, LA...  10.2 us
    unnamed x34, local copies, waits for them, and re-layouts  7.48 us
  transfers between devices with their start and end apart: 4, of which 0 were waited for; matrix products, arithmetic and copies ran while one was open for 0% of the time, Pallas kernels for 33%

profile of v2, /device:TPU:30, one launch (start us, length us, event | category | flops | bytes accessed | tf_op | source)
XLA Modules:
  0.0 101.9 jit_solution(10552056379267188597)
XLA Ops:
  0.6 0.0 copy-start.3
  0.6 0.9 copy-done.3
  1.6 0.0 copy-start.5
  1.6 0.9 copy-done.5
  2.5 0.0 copy-start.7
  2.5 0.9 copy-done.7
  3.4 0.0 copy-start.10
  3.4 0.7 copy-done.10
  4.0 0.0 copy-start.12
  4.0 0.7 copy-done.12
  4.7 0.0 copy-start.13
  4.7 0.7 copy-done.13
  5.4 0.0 copy-start.14
  5.4 0.7 copy-done.14
  6.1 0.0 copy-start.16
  6.1 0.7 copy-done.16
  6.8 0.0 copy-start.2
  6.8 0.0 copy-start.6
  6.8 0.0 copy-start.9
  6.8 0.0 copy-start.11
  6.8 37.7 %edge_columns.1 = (s32[8,256]{1,0:T(8,128)S(1)}, f32[8,256]{1,0:T(8,128)S(1)}, f32[8,256]{1,0:T(8,128)S(1)}, f32[130,256]{1,0:T(8,128)S(1)}, f32[130,32,128]{2,1...) custom-call(s32[32]{0:T(128)S(1)} %copy-done.10, ...), custom_call_target="tpu_custom_call" | custom-call | tf_op jit(solution)/shard_map/edge_columns/pallas_call | solution.py:615
  44.5 1.3 %collective-permute-start = (f32[1176,128]{1,0:T(8,128)S(1)}, f32[1176,128]{1,0:T(8,128)S(1)}, u32[]{:S(2)}, u32[]{:S(2)}) collective-permute-start(f32[1176,128]{1,0:T(8,128)S(1)} %get-tuple-element.22.s1), channel_id=1, source_target_pairs={{0,8},{2,10},{4,12},{6,14},{8,16},{10,18},{12,20},{14,22},{16,24},... | collective-permute-start | bytes 1806344 | tf_op jit(solution)/shard_map/ppermute | solution.py:576
  45.8 4.6 %collective-permute-start.1 = (f32[1176,128]{1,0:T(8,128)S(1)}, f32[1176,128]{1,0:T(8,128)S(1)}, u32[]{:S(2)}, u32[]{:S(2)}) collective-permute-start(f32[1176,128]{1,0:T(8,128)S(1)} %get-tuple-element.23.s0), channel_id=1, source_target_pairs={{8,0},{10,2},{12,4},{14,6},{16,8},{18,10},{20,12},{22,14},{24,16},... | collective-permute-start | bytes 1806344 | tf_op jit(solution)/shard_map/ppermute | solution.py:576
  50.4 0.0 copy-done.2
  50.4 0.0 copy-done.6
  50.4 0.0 copy-done.9
  50.4 0.0 copy-done.11
  50.5 18.0 %inner_columns.1 = (f32[130,32,128]{2,1,0:T(8,128)}, f32[1176,256]{1,0:T(8,128)S(1)}, bf16[256,256]{1,0:T(8,128)(2,1)S(1)}, bf16[256,256]{1,0:T(8,128)(2,1)S(1)}) custom-call(s32[8,256]{1,0:T(8,128)S(1)} %get-tuple-element.24.ilist, f32[8,256]{1,0:T(8,128)S(1)} %get-tuple-element.25.ylist, s32[32]{0:T(128)S(1)} %copy-done.10, ...), custom_call_target="tpu_custom_call" | custom-call | tf_op jit(solution)/shard_map/inner_columns/pallas_call | solution.py:661
  68.4 0.0 copy-start.1
  68.4 0.0 collective-permute-done.west.h0
  68.4 0.0 collective-permute-done.1.east.h1
  68.5 0.7 y_edges.1
  69.1 1.9 %collective-permute-start.2 = (f32[1176,128]{1,0:T(8,128)S(1)}, f32[1176,128]{1,0:T(8,128)S(1)}, u32[]{:S(2)}, u32[]{:S(2)}) collective-permute-start(f32[1176,128]{1,0:T(8,128)S(1)} %get-tuple-element.34), channel_id=1, source_target_pairs={{0,2},{2,4},{4,6},{6,8},{8,10},{10,12},{12,14},{14,16},{16,18},{18... | collective-permute-start | bytes 1806344 | tf_op jit(solution)/shard_map/ppermute | solution.py:576
  71.1 3.6 %collective-permute-start.3 = (f32[1176,128]{1,0:T(8,128)S(1)}, f32[1176,128]{1,0:T(8,128)S(1)}, u32[]{:S(2)}, u32[]{:S(2)}) collective-permute-start(f32[1176,128]{1,0:T(8,128)S(1)} %get-tuple-element.35), channel_id=1, source_target_pairs={{2,0},{4,2},{6,4},{8,6},{10,8},{12,10},{14,12},{16,14},{18,16},{20... | collective-permute-start | bytes 1806344 | tf_op jit(solution)/shard_map/ppermute | solution.py:576
  74.7 0.0 copy-done.1
  74.7 0.0 copy-start.4
  74.7 0.0 copy-start.8
  74.8 0.0 copy-start.15
  74.8 15.4 %inner_later.1.t_b = f32[130,32,128]{2,1,0:T(8,128)S(1)} custom-call(s32[8,256]{1,0:T(8,128)S(1)} %get-tuple-element.24.ilist, f32[8,256]{1,0:T(8,128)S(1)} %get-tuple-element.25.ylist, s32[32]{0:T(128)S(1)} %copy-done.10, f32[8,256]{1,0:T(8,128)S(1)} %get-tuple-element.26.counts, f32[4,1080,128]{2,1,0:T(8,128)} %get-tuple-element.29.held_b, ...), custom_call_target="tpu_custom_call" | custom-call | tf_op jit(solution)/shard_map/inner_later/pallas_call | solution.py:686
  90.2 0.0 copy-start
  90.2 1.3 %copy-done = f32[130,32,128]{2,1,0:T(8,128)} copy-done((f32[130,32,128]{2,1,0:T(8,128)}, f32[130,32,128]{2,1,0:T(8,128)S(1)}, u32[]{:S(2)}) %copy-start) | copy-done | bytes 2129944
  91.5 0.0 collective-permute-done.2.h2
  91.5 0.0 collective-permute-done.3.h3
  91.5 0.0 copy-done.4
  91.6 0.0 copy-done.8
  91.6 0.0 copy-done.15
  91.6 10.2 %advection.1 = (f32[32,130,2,128]{3,2,1,0:T(2,128)}, f32[130,2,128]{2,1,0:T(2,128)}) custom-call(f32[130,256]{1,0:T(8,128)S(1)} %get-tuple-element.21.conc, f32[1176,128]{1,0:T(8,128)S(1)} %collective-permute-done.west.h0, f32[1176,128]{1,0:T(8,128)S(1)} %collective-permute-done.1.east.h1, f32[1176,128]{1,0:T(8,128)S(1)} %collective-permute-done.2.h2, ...), custom_call_target="tpu_custom_call" | custom-call | tf_op jit(solution)/shard_map/advection/pallas_call | solution.py:696
Async XLA Ops:
  0.6 0.9 copy-start.3
  1.6 0.9 copy-start.5
  2.5 0.9 copy-start.7
  3.4 0.7 copy-start.10
  4.0 0.7 copy-start.12
  4.7 0.7 copy-start.13
  5.4 0.7 copy-start.14
  6.1 0.7 copy-start.16
  6.8 43.7 %copy-start.2 = (s32[768,3]{1,0:T(8,128)S(1)}, s32[768,3]{1,0:T(8,128)}, u32[]{:S(2)}) copy-start(s32[768,3]{1,0:T(8,128)} %constant.16.clone.side_in) | copy-start | bytes 27652
  6.8 43.7 %copy-start.6 = (bf16[256,256]{1,0:T(8,128)(2,1)S(1)}, bf16[256,256]{1,0:T(8,128)(2,1)}, u32[]{:S(2)}) copy-start(bf16[256,256]{1,0:T(8,128)(2,1)} %constant.15.clone.side_pick) | copy-start | bytes 393220
  6.8 43.7 %copy-start.9 = (f32[2,1,256]{2,1,0:T(1,128)S(1)}, f32[2,1,256]{2,1,0:T(1,128)}, u32[]{:S(2)}) copy-start(f32[2,1,256]{2,1,0:T(1,128)} %param.20) | copy-start | bytes 6148
  6.8 43.7 %copy-start.11 = (s32[3,256]{1,0:T(4,128)S(1)}, s32[3,256]{1,0:T(4,128)}, u32[]{:S(2)}) copy-start(s32[3,256]{1,0:T(4,128)} %constant.17.clone.side_out) | copy-start | bytes 9220
  44.5 23.9 %collective-permute-start = (f32[1176,128]{1,0:T(8,128)S(1)}, f32[1176,128]{1,0:T(8,128)S(1)}, u32[]{:S(2)}, u32[]{:S(2)}) collective-permute-start(f32[1176,128]{1,0:T(8,128)S(1)} %get-tuple-element.22.s1), channel_id=1, source_target_pairs={{0,8},{2,10},{4,12},{6,14},{8,16},{10,18},{12,20},{14,22},{16,24},... | collective-permute-start | bytes 1806344 | tf_op jit(solution)/shard_map/ppermute | solution.py:576
  45.8 22.6 %collective-permute-start.1 = (f32[1176,128]{1,0:T(8,128)S(1)}, f32[1176,128]{1,0:T(8,128)S(1)}, u32[]{:S(2)}, u32[]{:S(2)}) collective-permute-start(f32[1176,128]{1,0:T(8,128)S(1)} %get-tuple-element.23.s0), channel_id=1, source_target_pairs={{8,0},{10,2},{12,4},{14,6},{16,8},{18,10},{20,12},{22,14},{24,16},... | collective-permute-start | bytes 1806344 | tf_op jit(solution)/shard_map/ppermute | solution.py:576
  68.4 6.3 %copy-start.1 = (f32[130,32,128]{2,1,0:T(8,128)S(1)}, f32[130,32,128]{2,1,0:T(8,128)}, u32[]{:S(2)}) copy-start(f32[130,32,128]{2,1,0:T(8,128)} %get-tuple-element.37.t_b) | copy-start | bytes 6389764
  69.1 22.4 %collective-permute-start.2 = (f32[1176,128]{1,0:T(8,128)S(1)}, f32[1176,128]{1,0:T(8,128)S(1)}, u32[]{:S(2)}, u32[]{:S(2)}) collective-permute-start(f32[1176,128]{1,0:T(8,128)S(1)} %get-tuple-element.34), channel_id=1, source_target_pairs={{0,2},{2,4},{4,6},{6,8},{8,10},{10,12},{12,14},{14,16},{16,18},{18... | collective-permute-start | bytes 1806344 | tf_op jit(solution)/shard_map/ppermute | solution.py:576
  71.1 20.5 %collective-permute-start.3 = (f32[1176,128]{1,0:T(8,128)S(1)}, f32[1176,128]{1,0:T(8,128)S(1)}, u32[]{:S(2)}, u32[]{:S(2)}) collective-permute-start(f32[1176,128]{1,0:T(8,128)S(1)} %get-tuple-element.35), channel_id=1, source_target_pairs={{2,0},{4,2},{6,4},{8,6},{10,8},{12,10},{14,12},{16,14},{18,16},{20... | collective-permute-start | bytes 1806344 | tf_op jit(solution)/shard_map/ppermute | solution.py:576
  74.7 16.8 %copy-start.4 = (s32[384,2]{1,0:T(8,128)S(1)}, s32[384,2]{1,0:T(8,128)}, u32[]{:S(2)}) copy-start(s32[384,2]{1,0:T(8,128)} %constant.18.clone.entries) | copy-start | bytes 9220
  74.7 16.8 %copy-start.8 = (s32[256,2]{1,0:T(8,128)S(1)}, s32[256,2]{1,0:T(8,128)}, u32[]{:S(2)}) copy-start(s32[256,2]{1,0:T(8,128)} %constant.19.clone.cells) | copy-start | bytes 6148
  74.8 16.8 %copy-start.15 = (s32[2,256]{1,0:T(2,128)S(1)}, s32[2,256]{1,0:T(2,128)}, u32[]{:S(2)}) copy-start(s32[2,256]{1,0:T(2,128)} %constant.20.clone.cells_rows) | copy-start | bytes 6148
  90.2 1.3 %copy-start = (f32[130,32,128]{2,1,0:T(8,128)}, f32[130,32,128]{2,1,0:T(8,128)S(1)}, u32[]{:S(2)}) copy-start(f32[130,32,128]{2,1,0:T(8,128)S(1)} %inner_later.1.t_b) | copy-start | bytes 6389764
